TPU v7x, 512 devices: a whole 4x4x16 slice. The times are simulated.
512 devices in a mesh: region: 8 (over x, y_hi), pos: 64 (over z, y_lo, core).
Axes of the slice: x: 4, y: 4 (y_hi: 2, y_lo: 2; y = y_hi * 2 + y_lo), z: 16, core: 2. Of those that a mesh axis runs over, the one named last changes fastest.
Arguments:
- object_real: bfloat16 [3, 2048, 256], P(None, ('region', 'pos')), may hold values from 0.5 to 1.5
- object_imag: bfloat16 [3, 2048, 256], P(None, ('region', 'pos')), may hold values from -1.1953125 to 1.1953125
- probe_real: float32 [128, 128], replicated, may hold values from -4 to 4
- probe_imag: float32 [128, 128], replicated, may hold values from -4 to 4
- patterns: bfloat16 [8, 768, 128, 128], P('region', 'pos'), may hold values from 0 to 2
- offsets: int32 [8, 768, 2], P('region', 'pos'), may hold values from 0 to 255, as said below
- counts: int32 [8, 64], P('region', 'pos'), may hold values from 1 to 12, as said below
Outputs:
- grad_real: float32 [3, 2048, 256], P(None, ('region', 'pos'))
- grad_imag: float32 [3, 2048, 256], P(None, ('region', 'pos'))
Inputs may be any that keep to these rules, and one draw needn't show every extreme that they name: offsets[..., 0] lies in 0..255 and reaches 255 in every draw; offsets[..., 1] lies in 0..128. `counts`: every device has at least one live slot; some device has all 12 live in every draw.
All inputs are finite; a program needn't handle non-finite values.
Results may differ from a plain program's by a relative error of at most 0.0024.
Values may be sent and summed in bfloat16 or wider, within the bound.
No kernel may reach another device: no remote copies, remote signals or barrier semaphores. Data moves between devices by JAX's collectives and lax.ppermute only.
A program may use at most 64 MiB of HBM per device.

v0:
```python
import math

import jax
import jax.numpy as jnp
from jax import lax
from jax.sharding import PartitionSpec as P

FRESNEL = 12.0


def from_behind(block, axis, distance):
    devices = range(lax.axis_size(axis))
    route = [((i - distance) % len(devices), i) for i in devices]
    return lax.ppermute(block, axis, route)


def product(left, right):
    return jnp.dot(left, right, precision=lax.Precision.HIGHEST, preferred_element_type=jnp.float32)


def dft_tables(width):
    index = jnp.arange(width, dtype=jnp.int32)
    phases = index[:, None] * index[None, :] % width
    angle = 2.0 * math.pi / width * phases.astype(jnp.float32)
    factor = 1.0 / math.sqrt(width)
    return (jnp.cos(angle) * factor, -jnp.sin(angle) * factor)


def fresnel_kernel(width):
    index = jnp.arange(width, dtype=jnp.int32)
    freq = ((index + width // 2) % width - width // 2).astype(jnp.float32) / width
    phase = -math.pi * FRESNEL * (freq[:, None] * freq[:, None] + freq[None, :] * freq[None, :])
    return (jnp.cos(phase), jnp.sin(phase))


def complex_mul(first_pair, second_pair):
    return (
        first_pair[0] * second_pair[0] - first_pair[1] * second_pair[1],
        first_pair[0] * second_pair[1] + first_pair[1] * second_pair[0],
    )


def conjugate(pair):
    return (pair[0], -pair[1])


def transform(field, tables, inverse):
    table_real, table_imag = tables
    if inverse:
        table_imag = -table_imag
    left_real = product(table_real, field[0]) - product(table_imag, field[1])
    left_imag = product(table_real, field[1]) + product(table_imag, field[0])
    out_real = product(left_real, table_real) - product(left_imag, table_imag)
    out_imag = product(left_real, table_imag) + product(left_imag, table_real)
    return (out_real, out_imag)


def propagate(field, tables, kernel):
    spectrum = transform(field, tables, False)
    return transform(complex_mul(kernel, spectrum), tables, True)


def patch_gradient(layers, probe, measured, tables, kernel):
    slices = len(layers)
    waves = []
    wave = probe
    exit_wave = probe
    for layer in range(slices):
        waves.append(wave)
        exit_wave = complex_mul(wave, layers[layer])
        if layer < slices - 1:
            wave = propagate(exit_wave, tables, kernel)
    farfield = transform(exit_wave, tables, False)
    intensity = farfield[0] * farfield[0] + farfield[1] * farfield[1]
    misfit = intensity - measured
    backward = transform((misfit * farfield[0], misfit * farfield[1]), tables, True)
    grads = [None] * slices
    back_kernel = conjugate(kernel)
    for layer in range(slices - 1, -1, -1):
        grads[layer] = complex_mul(conjugate(waves[layer]), backward)
        if layer > 0:
            backward = propagate(
                complex_mul(conjugate(layers[layer]), backward), tables, back_kernel
            )
    return (jnp.stack([pair[0] for pair in grads]), jnp.stack([pair[1] for pair in grads]))


def local(object_real, object_imag, probe_real, probe_imag, patterns, offsets, counts):
    slices = object_real.shape[0]
    columns = object_real.shape[2]
    width = probe_real.shape[0]
    capacity = patterns.shape[1]
    pos_count = lax.axis_size("pos")
    tile_real, tile_imag = (
        lax.all_gather(object_real, "pos", axis=1, tiled=True),
        lax.all_gather(object_imag, "pos", axis=1, tiled=True),
    )
    next_real, next_imag = from_behind((tile_real[:, :width], tile_imag[:, :width]), "region", -1)
    region_rows = tile_real.shape[1]
    extended_real = jnp.concatenate([tile_real, next_real], axis=1)
    extended_imag = jnp.concatenate([tile_imag, next_imag], axis=1)
    work_patterns = patterns[0]
    work_offsets = offsets[0]
    workload = counts[0, 0]
    tables = dft_tables(width)
    kernel = fresnel_kernel(width)
    probe = (probe_real, probe_imag)
    scale = 1.0 / math.sqrt(capacity * pos_count)

    def visit(number, carry):
        grad_real, grad_imag = carry
        row_start = work_offsets[number, 0]
        col_start = work_offsets[number, 1]
        start = (jnp.int32(0), row_start, col_start)
        layer_real = lax.dynamic_slice(extended_real, start, (slices, width, width)).astype(
            jnp.float32
        )
        layer_imag = lax.dynamic_slice(extended_imag, start, (slices, width, width)).astype(
            jnp.float32
        )
        layers = [(layer_real[layer], layer_imag[layer]) for layer in range(slices)]
        measured = lax.dynamic_index_in_dim(work_patterns, number, 0, keepdims=False).astype(
            jnp.float32
        )
        term_real, term_imag = patch_gradient(layers, probe, measured, tables, kernel)
        old_real = lax.dynamic_slice(grad_real, start, (slices, width, width))
        old_imag = lax.dynamic_slice(grad_imag, start, (slices, width, width))
        grad_real = lax.dynamic_update_slice(grad_real, old_real + scale * term_real, start)
        grad_imag = lax.dynamic_update_slice(grad_imag, old_imag + scale * term_imag, start)
        return (grad_real, grad_imag)

    zeros = jnp.zeros((slices, region_rows + width, columns), jnp.float32)
    grad_real, grad_imag = lax.fori_loop(0, workload, visit, (zeros, zeros))
    carried_real, carried_imag = (
        from_behind(grad_real[:, region_rows:].astype(jnp.bfloat16), "region", 1).astype(
            jnp.float32
        ),
        from_behind(grad_imag[:, region_rows:].astype(jnp.bfloat16), "region", 1).astype(
            jnp.float32
        ),
    )
    band_grad_real = grad_real[:, :region_rows].at[:, :width].add(carried_real)
    band_grad_imag = grad_imag[:, :region_rows].at[:, :width].add(carried_imag)
    out_real, out_imag = (
        lax.psum_scatter(band_grad_real, "pos", scatter_dimension=1, tiled=True),
        lax.psum_scatter(band_grad_imag, "pos", scatter_dimension=1, tiled=True),
    )
    return (out_real, out_imag)


def solution(mesh):
    return jax.shard_map(
        local,
        mesh=mesh,
        in_specs=(
            P(None, ("region", "pos"), None),
            P(None, ("region", "pos"), None),
            P(),
            P(),
            P("region", "pos", None, None),
            P("region", "pos", None),
            P("region", "pos"),
        ),
        out_specs=(P(None, ("region", "pos"), None), P(None, ("region", "pos"), None)),
        check_vma=False,
    )
```

profile of v0, /device:TPU:6, one launch (start us, length us, event | category | flops | bytes accessed | tf_op | source)
XLA Modules:
  0.0 1352.9 jit_solution(1624528338292926161)
XLA Ops:
  7.9 71.2 %all_gather.6 = bf16[3,256,256]{2,0,1:T(4,128)(2,1)S(1)} all-gather(bf16[3,4,256]{2,0,1:T(4,128)(2,1)S(1)} %copy.9), channel_id=1, replica_groups=mesh['region'=8,'pos'=64] {'pos'}, dimensions={1}, use_global_device_ids=true | all-gather | bytes 399360 | tf_op jit(solution)/shard_map/all_gather | solution.py:95
  79.2 5.0 collective-permute-start
  84.9 64.3 %all_gather.7 = bf16[3,256,256]{2,0,1:T(4,128)(2,1)S(1)} all-gather(bf16[3,4,256]{2,0,1:T(4,128)(2,1)S(1)} %copy.10), channel_id=1, replica_groups=mesh['region'=8,'pos'=64] {'pos'}, dimensions={1}, use_global_device_ids=true | all-gather | bytes 399360 | tf_op jit(solution)/shard_map/all_gather | solution.py:96
  149.3 1.9 collective-permute-start.1
  151.9 9.4 collective-permute-done.1
  163.5 488.0 %while.18 = (s32[]{:T(128)}, f32[3,384,256]{2,1,0:T(8,128)S(1)}, f32[3,384,256]{2,1,0:T(8,128)S(1)}, s32[]{:T(128)}, s32[12,2]{0,1:T(2,128)S(1)}, /*index=5*/bf1...) while((s32[]{:T(128)}, f32[3,384,256]{2,1,0:T(8,128)S(1)}, ...), condition=%wide.region_1.2_spmd.clone.clone.clone, body=%wide.region_0.1_spmd.clone.clone.clone.sunk | while | flops 2037743616 | bytes 19472712 | solution.py:133
  184.1 1.5 convolution_add_fusion.43
  193.0 1.3 fusion.864
  194.3 1.3 convolution_add_fusion.46
  195.5 1.3 fusion.862
  196.8 1.3 convolution_subtract_fusion.47
  218.6 2.8 dynamic_update_slice.17
  221.4 2.8 dynamic_update_slice.16
  253.3 1.3 fusion.864
  254.5 1.3 convolution_add_fusion.46
  255.8 1.3 fusion.862
  257.1 1.3 convolution_subtract_fusion.47
  279.1 2.7 dynamic_update_slice.17
  281.8 2.7 dynamic_update_slice.16
  304.9 1.2 convolution_add_fusion.43
  313.6 1.3 fusion.864
  314.9 1.3 convolution_add_fusion.46
  316.2 1.3 fusion.862
  317.5 1.3 convolution_subtract_fusion.47
  339.2 3.0 dynamic_update_slice.17
  342.3 3.0 dynamic_update_slice.16
  374.4 1.3 fusion.864
  375.7 1.3 convolution_add_fusion.46
  376.9 1.3 fusion.862
  378.2 1.3 convolution_subtract_fusion.47
  400.2 3.1 dynamic_update_slice.17
  403.3 3.1 dynamic_update_slice.16
  426.7 1.2 convolution_add_fusion.43
  435.4 1.3 fusion.864
  436.7 1.3 convolution_add_fusion.46
  437.9 1.3 fusion.862
  439.2 1.3 convolution_subtract_fusion.47
  461.0 3.0 dynamic_update_slice.17
  464.0 3.0 dynamic_update_slice.16
  496.0 1.3 fusion.864
  497.2 1.3 convolution_add_fusion.46
  498.5 1.3 fusion.862
  499.8 1.3 convolution_subtract_fusion.47
  521.8 2.8 dynamic_update_slice.17
  524.6 2.8 dynamic_update_slice.16
  547.7 1.2 convolution_add_fusion.43
  556.4 1.3 fusion.864
  557.7 1.3 convolution_add_fusion.46
  559.0 1.3 fusion.862
  560.3 1.3 convolution_subtract_fusion.47
  582.0 2.9 dynamic_update_slice.17
  584.9 2.9 dynamic_update_slice.16
  616.8 1.3 fusion.864
  618.1 1.3 convolution_add_fusion.46
  619.4 1.3 fusion.862
  620.6 1.3 convolution_subtract_fusion.47
  642.6 3.1 dynamic_update_slice.17
  645.7 3.1 dynamic_update_slice.16
  651.6 61.9 %collective-permute-start.3 = (bf16[3,128,256]{2,1,0:T(8,128)(2,1)S(1)}, bf16[3,128,256]{2,1,0:T(8,128)(2,1)S(1)}, u32[]{:S(2)}, u32[]{:S(2)}) collective-permute-start(bf16[3,128,256]{2,1,0:T(8,128)(2,1)S(1)} %slice.180), channel_id=1, source_target_pairs={{448,0},{0,64},{64,128},{128,192},{192,256},{256,320},{320,384},{3... | collective-permute-start | bytes 589832 | tf_op jit(solution)/shard_map/ppermute | solution.py:14
  713.7 1.9 collective-permute-start.2
  715.6 64.7 %collective-permute-done.3 = bf16[3,128,256]{2,1,0:T(8,128)(2,1)S(1)} collective-permute-done((bf16[3,128,256]{2,1,0:T(8,128)(2,1)S(1)}, bf16[3,128,256]{2,1,0:T(8,128)(2,1)S(1)}, u32[]{:S(2)}, u32[]{:S(2)}) %collective-permute-start.3) | collective-permute-done | bytes 196640 | tf_op jit(solution)/shard_map/ppermute | solution.py:14
  783.4 1.3 dynamic-slice.16
  785.3 559.1 %all-reduce.5.cloned.1.call-done = (f32[3,256,256]{2,1,0:T(8,128)}, f32[3,256,256]{2,1,0:T(8,128)}) async-done(((f32[3,256,256]{2,1,0:T(8,128)}, f32[3,256,256]{2,1,0:T(8,128)}), (f32[3,256,256]{2,1,0:T(8,128)}, f32[3,256,256]{2,1,0:T(8,128)})) %all-reduce.5.cloned.1.call-update) | async-done | bytes 1572880
  1344.4 1.4 constant_dynamic-slice_fusion.2
  (676 shorter events, 356.6 us)
Async XLA Ops:
  7.2 144.1 %copy-start.3 = (f32[128,128]{1,0:T(8,128)S(1)}, f32[128,128]{1,0:T(8,128)}, u32[]{:S(2)}) copy-start(f32[128,128]{1,0:T(8,128)} %param.16) | copy-start | bytes 196612
  7.2 1337.2 %all-reduce.5.cloned.1.call-start = ((), (), s32[]{:S(2)}) async-start(), calls=%async_computation | async-start | bytes 3145728
  79.2 72.1 %collective-permute-start = (bf16[3,128,256]{2,0,1:T(4,128)(2,1)S(1)}, bf16[3,128,256]{2,0,1:T(4,128)(2,1)S(1)}, u32[]{:S(2)}, u32[]{:S(2)}) collective-permute-start(bf16[3,128,256]{2,0,1:T(4,128)(2,1)S(1)} %slice.126), channel_id=1, source_target_pairs={{64,0},{128,64},{192,128},{256,192},{320,256},{384,320},{448,384},... | collective-permute-start | bytes 589832 | tf_op jit(solution)/shard_map/ppermute | solution.py:14
  149.3 12.0 collective-permute-start.1
  162.7 0.8 copy-start
  162.7 0.8 copy-start.4
  651.6 128.7 %collective-permute-start.3 = (bf16[3,128,256]{2,1,0:T(8,128)(2,1)S(1)}, bf16[3,128,256]{2,1,0:T(8,128)(2,1)S(1)}, u32[]{:S(2)}, u32[]{:S(2)}) collective-permute-start(bf16[3,128,256]{2,1,0:T(8,128)(2,1)S(1)} %slice.180), channel_id=1, source_target_pairs={{448,0},{0,64},{64,128},{128,192},{192,256},{256,320},{320,384},{3... | collective-permute-start | bytes 589832 | tf_op jit(solution)/shard_map/ppermute | solution.py:14
  713.7 68.8 %collective-permute-start.2 = (bf16[3,128,256]{2,1,0:T(8,128)(2,1)S(1)}, bf16[3,128,256]{2,1,0:T(8,128)(2,1)S(1)}, u32[]{:S(2)}, u32[]{:S(2)}) collective-permute-start(bf16[3,128,256]{2,1,0:T(8,128)(2,1)S(1)} %slice.181), channel_id=1, source_target_pairs={{448,0},{0,64},{64,128},{128,192},{192,256},{256,320},{320,384},{3... | collective-permute-start | bytes 589832 | tf_op jit(solution)/shard_map/ppermute | solution.py:14
  780.4 0.9 copy-start.2
  782.5 0.9 copy-start.1
Sparse Core Ops, SparseCore 0:
  783.5 560.8 all-reduce.4
where the time goes:
time: 1360 us; the launch traced here: 1350 us
  waiting for transfers between devices  634 us (47%)
  matrix products  379 us (28%)
  blocking collectives  136 us (10%)
  starting transfers between devices  70.8 us (5%)
  local copies, waits for them, and re-layouts  59.7 us (4%)
  loops' own time  46.3 us (3%)
  between operations  15.1 us (1%)
    unnamed x2, waiting for transfers between devices  559 us
    dot_general x640, matrix products, product(): jnp.dot(left, right, precision=lax.Precision.HIGHEST, preferred_element_t...  379 us
    ppermute x4, waiting for transfers between devices, from_behind(): return lax.ppermute(block, axis, route)  75.3 us
    all_gather x1, blocking collectives, local(): lax.all_gather(object_real, 'pos', axis=1, tiled=True)  71.2 us
    ppermute x4, starting transfers between devices, from_behind(): return lax.ppermute(block, axis, route)  70.7 us
    all_gather x1, blocking collectives, local(): lax.all_gather(object_imag, 'pos', axis=1, tiled=True)  64.3 us
    another operation x1, loops' own time, local(): grad_real, grad_imag = lax.fori_loop(0, workload, visit, (zeros, zeros))  46.3 us
  transfers between devices with their start and end apart: 5, of which 4 were waited for; matrix products, arithmetic and copies ran while one was open for 0% of the time, Pallas kernels for 0%

commit v1 on v0

v1 whole, which is shorter than its diff:
```python
import functools
import math

import jax
import jax.numpy as jnp
import numpy as np
from jax import lax
from jax.experimental import pallas as pl
from jax.experimental.pallas import tpu as pltpu
from jax.sharding import Mesh
from jax.sharding import PartitionSpec as P

FRESNEL = 12.0
GROUP = 4
PROP, DFT = 0, 2
POS = ("z", "yl", "core")


def block_tables(width):
    index = np.arange(width)
    turns = index[:, None] * index[None, :] % width
    dft = np.exp(-2j * np.pi * turns / width) / np.sqrt(width)
    freq = np.fft.fftfreq(width)
    phase = np.exp(-1j * np.pi * FRESNEL * freq * freq)
    prop = np.conj(dft) @ (phase[:, None] * dft)
    pieces = []
    for matrix in (prop, dft):
        right = np.block([[matrix.real, matrix.imag], [-matrix.imag, matrix.real]])
        for table in (right, right.T):
            high = table.astype(np.float32).astype(jnp.bfloat16)
            low = (table - high.astype(np.float64)).astype(np.float32).astype(jnp.bfloat16)
            pieces.append(np.stack([high, low]))
    return np.stack(pieces)


def split(value):
    high = value.astype(jnp.bfloat16)
    low = (value - high.astype(jnp.float32)).astype(jnp.bfloat16)
    return high, low


def dot(first, second):
    return jnp.dot(first, second, preferred_element_type=jnp.float32)


def left(table_ref, which, real, imag):
    field = jnp.concatenate(
        [jnp.concatenate(real, axis=1), jnp.concatenate(imag, axis=1)], axis=0
    )
    high, low = split(field)
    table_high, table_low = table_ref[which, 0], table_ref[which, 1]
    out = dot(table_high, high) + dot(table_low, high) + dot(table_high, low)
    w = real[0].shape[0]
    spans = [slice(k * w, (k + 1) * w) for k in range(len(real))]
    return [out[:w, s] for s in spans], [out[w:, s] for s in spans]


def right(table_ref, which, real, imag):
    field = jnp.concatenate(
        [jnp.concatenate([r, i], axis=1) for r, i in zip(real, imag)], axis=0
    )
    high, low = split(field)
    table_high, table_low = table_ref[which, 0], table_ref[which, 1]
    out = dot(high, table_high) + dot(high, table_low) + dot(low, table_high)
    w = real[0].shape[0]
    spans = [slice(k * w, (k + 1) * w) for k in range(len(real))]
    return [out[s, :w] for s in spans], [out[s, w:] for s in spans]


def transform(table_ref, base, adjoint, field):
    flip = 1 if adjoint else 0
    return right(table_ref, base + flip, *left(table_ref, base + 1 - flip, *field))


def mul(first, second):
    real = [p * r - q * s for p, q, r, s in zip(*first, *second)]
    imag = [p * s + q * r for p, q, r, s in zip(*first, *second)]
    return real, imag


def conj_mul(first, second):
    real = [p * r + q * s for p, q, r, s in zip(*first, *second)]
    imag = [p * s - q * r for p, q, r, s in zip(*first, *second)]
    return real, imag


def slots_kernel(
    scale,
    place_ref,
    off_ref,
    cnt_ref,
    probe_real_ref,
    probe_imag_ref,
    pat_ref,
    tab_ref,
    own_near_ref,
    own_far_ref,
    next_near_ref,
    next_far_ref,
    keep_ref,
    send_ref,
    keep_next_ref,
    send_next_ref,
    obj_ref,
    grad_ref,
):
    w = probe_real_ref.shape[0]
    slots = pat_ref.shape[0]
    slices = obj_ref.shape[1]
    half = 4
    yl = place_ref[0]
    first_core = place_ref[1] == 0
    grad_ref[...] = jnp.zeros_like(grad_ref)
    top = lax.broadcasted_iota(jnp.int32, (2 * half, w), 0) < half

    def unpack(near_ref, far_ref, first_row):
        def place(z, _):
            for y in range(2):
                row = first_row + (2 * z + lax.rem(y + yl, 2)) * 2 * half
                row = pl.multiple_of(row, 2 * half)
                near = near_ref[y, z].astype(jnp.float32)
                far = far_ref[y, z].astype(jnp.float32)
                low = jnp.where(first_core, near, far)
                high = jnp.where(first_core, far, near)
                for s in range(slices):
                    for h in range(2):
                        k = (s * 2 + h) * 2 * half
                        a, b = low[k : k + 2 * half], high[k : k + 2 * half]
                        obj_ref[0, s, h, pl.ds(row, 2 * half), :] = jnp.where(
                            top, a, pltpu.roll(b, half, 0)
                        )
                        obj_ref[1, s, h, pl.ds(row, 2 * half), :] = jnp.where(
                            top, pltpu.roll(a, half, 0), b
                        )
            return 0

        lax.fori_loop(0, near_ref.shape[1], place, 0)

    def pack(keep_out, send_out, first_row):
        def place(z, _):
            for y in range(2):
                row = first_row + (2 * z + lax.rem(y + yl, 2)) * 2 * half
                row = pl.multiple_of(row, 2 * half)
                for s in range(slices):
                    for h in range(2):
                        k = (s * 2 + h) * 2 * half
                        real = grad_ref[0, s, h, pl.ds(row, 2 * half), :]
                        imag = grad_ref[1, s, h, pl.ds(row, 2 * half), :]
                        low = jnp.where(top, real, pltpu.roll(imag, half, 0))
                        high = jnp.where(top, pltpu.roll(real, half, 0), imag)
                        keep_out[y, z, k : k + 2 * half] = jnp.where(first_core, low, high)
                        send_out[y, z, k : k + 2 * half] = jnp.where(first_core, high, low)
            return 0

        lax.fori_loop(0, keep_out.shape[1], place, 0)

    band_rows = own_near_ref.shape[1] * 4 * half
    unpack(own_near_ref, own_far_ref, 0)
    unpack(next_near_ref, next_far_ref, band_rows)

    count = cnt_ref[0, 0]
    lane = lax.broadcasted_iota(jnp.int32, (w, w), 1)

    def visit(step, _):
        numbers = [jnp.minimum(step * GROUP + k, slots - 1) for k in range(GROUP)]
        rows = [off_ref[0, n, 0] for n in numbers]
        cols = [off_ref[0, n, 1] for n in numbers]
        weights = [
            jnp.where(step * GROUP + k < count, scale, 0.0).astype(jnp.float32)
            for k in range(GROUP)
        ]
        turn = [lax.rem(c, w) for c in cols]
        back_turn = [lax.rem(2 * w - c, w) for c in cols]

        def window(part, layer):
            found = []
            for k in range(GROUP):
                near = obj_ref[part, layer, 0, pl.ds(rows[k], w), :]
                after = obj_ref[part, layer, 1, pl.ds(rows[k], w), :]
                found.append(pltpu.roll(jnp.where(lane >= cols[k], near, after), back_turn[k], 1))
            return found

        layers = [(window(0, s), window(1, s)) for s in range(slices)]
        wave = ([probe_real_ref[...]] * GROUP, [probe_imag_ref[...]] * GROUP)
        waves = []
        for s in range(slices):
            waves.append(wave)
            leaving = mul(wave, layers[s])
            if s < slices - 1:
                wave = transform(tab_ref, PROP, False, leaving)
        far = transform(tab_ref, DFT, False, leaving)
        misfit = [
            r * r + i * i - pat_ref[n].astype(jnp.float32) for r, i, n in zip(*far, numbers)
        ]
        back = ([m * r for m, r in zip(misfit, far[0])], [m * i for m, i in zip(misfit, far[1])])
        back = transform(tab_ref, DFT, True, back)
        for s in range(slices - 1, -1, -1):
            term = conj_mul(waves[s], back)
            for part in range(2):
                for k in range(GROUP):
                    moved = pltpu.roll(term[part][k] * weights[k], turn[k], 1)
                    here = lane >= cols[k]
                    grad_ref[part, s, 0, pl.ds(rows[k], w), :] += jnp.where(here, moved, 0.0)
                    grad_ref[part, s, 1, pl.ds(rows[k], w), :] += jnp.where(here, 0.0, moved)
            if s > 0:
                back = transform(tab_ref, PROP, True, conj_mul(layers[s], back))
        return 0

    lax.fori_loop(0, lax.div(count + (GROUP - 1), GROUP), visit, 0)
    pack(keep_next_ref, send_next_ref, band_rows)
    pack(keep_ref, send_ref, 0)


def slots_call(scale, place, offsets, counts, probe, patterns, tables, own, following):
    slices = 3
    width = probe[0].shape[0]
    rows = (own[0].shape[1] + following[0].shape[1]) * 16
    vector = pl.BlockSpec(memory_space=pltpu.VMEM)
    scalar = pl.BlockSpec(memory_space=pltpu.SMEM)
    held = pltpu.VMEM((2, slices, 2, rows, width), jnp.float32)
    outs = [jax.ShapeDtypeStruct(x.shape, jnp.float32) for x in (own[0],) * 2 + (following[0],) * 2]
    return pl.pallas_call(
        functools.partial(slots_kernel, scale),
        out_shape=outs,
        in_specs=[scalar] * 3 + [vector] * 8,
        out_specs=[vector] * 4,
        scratch_shapes=[held, held],
        compiler_params=pltpu.CompilerParams(vmem_limit_bytes=56 * 1024 * 1024),
        name="slots",
    )(place, offsets, counts, *probe, patterns, tables, *own, *following)


def swap(block, axis):
    return lax.ppermute(block, axis, [(0, 1), (1, 0)])


def shift(block, distance):
    bands = lax.axis_size("region")
    return lax.ppermute(block, "region", [(i, (i + distance) % bands) for i in range(bands)])


def local(tables, object_real, object_imag, probe_real, probe_imag, patterns, offsets, counts):
    slices, rows, columns = object_real.shape
    width = probe_real.shape[0]
    halves = columns // width
    depth = lax.axis_size("z")
    below = depth * width // (depth * 4 * rows)
    packed = slices * halves * 2 * rows
    yl = lax.axis_index("yl")
    place = jnp.stack([yl, lax.axis_index("core")]).astype(jnp.int32)
    scale = 1.0 / math.sqrt(patterns.shape[1] * depth * 4)

    with jax.named_scope("gather"):
        block = jnp.stack([object_real, object_imag]).reshape(2, slices, rows, halves, width)
        block = block.transpose(1, 3, 0, 2, 4).reshape(1, packed, width)
        column = lax.all_to_all(
            jnp.broadcast_to(block, (depth, packed, width)), "z", 0, 0, tiled=True
        )
        following = shift(column[:below], -1)
        other = swap(column, "yl")
        own = jnp.stack([column, other])
        own_far = swap(own, "core")
        following = jnp.stack([following, swap(following, "yl")])
        following_far = swap(following, "core")

    keep, send, keep_next, send_next = slots_call(
        scale,
        place,
        offsets,
        counts,
        (probe_real, probe_imag),
        patterns[0],
        tables,
        (own, own_far),
        (following, following_far),
    )

    with jax.named_scope("reduce"):
        carried = keep_next + swap(send_next, "core")
        total = keep + swap(send, "core")
        carried = carried[0] + swap(carried[1], "yl")
        total = total[0] + swap(total[1], "yl")
        total = total.at[:below].add(shift(carried, 1))
        total = lax.all_to_all(total, "z", 0, 0, tiled=True).sum(0)
        total = total.reshape(slices, halves, 2, rows, width).transpose(2, 0, 3, 1, 4)
        total = total.reshape(2, slices, rows, columns)
    return total[0], total[1]


def solution(mesh):
    fine = Mesh(mesh.devices.reshape(mesh.shape["region"], -1, 2, 2), ("region",) + POS)
    everything = ("region",) + POS
    run = jax.shard_map(
        local,
        mesh=fine,
        in_specs=(
            P(),
            P(None, everything, None),
            P(None, everything, None),
            P(),
            P(),
            P("region", POS, None, None),
            P("region", POS, None),
            P("region", POS),
        ),
        out_specs=(P(None, everything, None), P(None, everything, None)),
        check_vma=False,
    )

    def whole(object_real, object_imag, probe_real, probe_imag, patterns, offsets, counts):
        tables = jnp.asarray(block_tables(probe_real.shape[0]))
        return run(
            tables, object_real, object_imag, probe_real, probe_imag, patterns, offsets, counts
        )

    return whole
```

time: 1360 us -> 136 us (0.10)
  the two profiles are of different devices: /device:TPU:6 before, /device:TPU:22 now
where the time goes in v1:
time: 136 us
  blocking collectives  58.9 us (43%)
  starting transfers between devices  35.6 us (26%)
  waiting for transfers between devices  24.9 us (18%)
  Pallas kernels  9.9 us (7%)
  local copies, waits for them, and re-layouts  2.93 us (2%)
  other arithmetic  2.03 us (1%)
  between operations  1.56 us (1%)
    all_to_all x1, blocking collectives, local(): lax.all_to_all(jnp.broadcast_to(block, (depth, packed, width)), 'z', 0, 0...  31.4 us
    ppermute x8, starting transfers between devices, swap(): return lax.ppermute(block, axis, [(0, 1), (1, 0)])  31.1 us
    all_to_all x1, blocking collectives, local(): total = lax.all_to_all(total, 'z', 0, 0, tiled=True).sum(0)  27.5 us
    ppermute x8, waiting for transfers between devices, swap(): return lax.ppermute(block, axis, [(0, 1), (1, 0)])  17.3 us
    pallas_call x1, Pallas kernels, slots_call(): pl.pallas_call(functools.partial(slots_kernel, scale), out_shape=outs, in...  9.9 us
    ppermute x2, waiting for transfers between devices, shift(): lax.ppermute(block, 'region', [(i, (i + distance) % bands) for i in range...  7.58 us
    ppermute x2, starting transfers between devices, shift(): lax.ppermute(block, 'region', [(i, (i + distance) % bands) for i in range...  4.46 us
  transfers between devices with their start and end apart: 10, of which 5 were waited for; matrix products, arithmetic and copies ran while one was open for 2% of the time, Pallas kernels for 0%

profile of v1, /device:TPU:22, one launch (start us, length us, event | category | flops | bytes accessed | tf_op | source)
XLA Modules:
  0.0 135.7 jit_solution(4515024408351175757)
XLA Ops:
  0.6 0.0 copy-start.5
  0.6 0.7 stack.39
  1.3 0.0 copy-done.5
  1.4 31.4 %all_to_all.10 = bf16[16,48,128]{2,1,0:T(8,128)(2,1)S(1)} all-to-all(bf16[16,48,128]{2,1,0:T(8,128)(2,1)S(1)} %broadcast_in_dim.8), channel_id=1, replica_groups=mesh['region'=8,'z'=16,'yl'=2,'core'=2] {'z'}, dimensions={0} | all-to-all | bytes 393216 | tf_op jit(solution)/shard_map/gather/all_to_all | solution.py:256
  32.9 3.2 %collective-permute-start = (bf16[16,48,128]{2,1,0:T(8,128)(2,1)S(1)}, bf16[16,48,128]{2,1,0:T(8,128)(2,1)S(1)}, u32[]{:S(2)}, u32[]{:S(2)}) collective-permute-start(bf16[16,48,128]{2,1,0:T(8,128)(2,1)S(1)} %all_to_all.10), channel_id=1, source_target_pairs={{0,2},{2,0},{1,3},{3,1},{4,6},{6,4},{5,7},{7,5},{8,10},{10,8},{9,1... | collective-permute-start | bytes 589832 | tf_op jit(solution)/shard_map/gather/ppermute | solution.py:234
  36.1 2.5 %collective-permute-start.2 = (bf16[8,48,128]{2,1,0:T(8,128)(2,1)S(1)}, bf16[8,48,128]{2,1,0:T(8,128)(2,1)S(1)}, u32[]{:S(2)}, u32[]{:S(2)}) collective-permute-start(bf16[8,48,128]{2,1,0:T(8,128)(2,1)S(1)} %slice.55), channel_id=1, source_target_pairs={{0,448},{64,0},{128,64},{192,128},{256,192},{320,256},{384,320},{4... | collective-permute-start | bytes 294920 | tf_op jit(solution)/shard_map/gather/ppermute | solution.py:239
  38.6 7.6 %collective-permute-done.2 = bf16[8,48,128]{2,1,0:T(8,128)(2,1)S(1)} collective-permute-done((bf16[8,48,128]{2,1,0:T(8,128)(2,1)S(1)}, bf16[8,48,128]{2,1,0:T(8,128)(2,1)S(1)}, u32[]{:S(2)}, u32[]{:S(2)}) %collective-permute-start.2) | collective-permute-done | bytes 98336 | tf_op jit(solution)/shard_map/gather/ppermute | solution.py:239
  46.2 2.6 %collective-permute-start.3 = (bf16[8,48,128]{2,1,0:T(8,128)(2,1)S(1)}, bf16[8,48,128]{2,1,0:T(8,128)(2,1)S(1)}, u32[]{:S(2)}, u32[]{:S(2)}) collective-permute-start(bf16[8,48,128]{2,1,0:T(8,128)(2,1)S(1)} %collective-permute-done.2), channel_id=1, source_target_pairs={{0,2},{2,0},{1,3},{3,1},{4,6},{6,4},{5,7},{7,5},{8,10},{10,8},{9,1... | collective-permute-start | bytes 294920 | tf_op jit(solution)/shard_map/gather/ppermute | solution.py:234
  48.8 0.0 collective-permute-done
  48.9 0.0 copy-start
  48.9 1.9 %collective-permute-start.1 = (bf16[2,16,48,128]{3,2,1,0:T(8,128)(2,1)S(1)}, bf16[2,16,48,128]{3,2,1,0:T(8,128)(2,1)S(1)}, u32[]{:S(2)}, u32[]{:S(2)}) collective-permute-start(bf16[2,16,48,128]{3,2,1,0:T(8,128)(2,1)S(1)} %pad_maximum_fusion.own_near_ref), channel_id=1, source_target_pairs={{0,1},{1,0},{2,3},{3,2},{4,5},{5,4},{6,7},{7,6},{8,9},{9,8},{10,11... | collective-permute-start | bytes 1179656 | tf_op jit(solution)/shard_map/gather/ppermute | solution.py:234
  50.8 1.9 %collective-permute-done.3 = bf16[8,48,128]{2,1,0:T(8,128)(2,1)S(1)} collective-permute-done((bf16[8,48,128]{2,1,0:T(8,128)(2,1)S(1)}, bf16[8,48,128]{2,1,0:T(8,128)(2,1)S(1)}, u32[]{:S(2)}, u32[]{:S(2)}) %collective-permute-start.3) | collective-permute-done | bytes 98336 | tf_op jit(solution)/shard_map/gather/ppermute | solution.py:234
  52.7 0.0 copy-start.1
  52.7 1.9 %collective-permute-start.4 = (bf16[2,8,48,128]{3,2,1,0:T(8,128)(2,1)S(1)}, bf16[2,8,48,128]{3,2,1,0:T(8,128)(2,1)S(1)}, u32[]{:S(2)}, u32[]{:S(2)}) collective-permute-start(bf16[2,8,48,128]{3,2,1,0:T(8,128)(2,1)S(1)} %pad_maximum_fusion.1.next_near_ref), channel_id=1, source_target_pairs={{0,1},{1,0},{2,3},{3,2},{4,5},{5,4},{6,7},{7,6},{8,9},{9,8},{10,11... | collective-permute-start | bytes 589832 | tf_op jit(solution)/shard_map/gather/ppermute | solution.py:234
  54.7 0.0 copy-start.6
  55.3 0.0 copy-done.6
  55.3 0.7 copy.13.off_ref
  56.0 0.6 pad_add_fusion.place_ref
  56.6 0.0 collective-permute-done.4.next_far_ref
  56.6 0.0 copy-start.4
  56.6 0.0 collective-permute-done.1.own_far_ref
  56.6 0.0 copy-start.3
  56.6 0.0 copy-done
  56.7 0.0 copy-done.1
  56.7 0.6 copy-done.4
  57.3 0.2 copy-done.3
  57.5 9.9 %slots.1 = (f32[2,16,48,128]{3,2,1,0:T(8,128)}, f32[2,16,48,128]{3,2,1,0:T(8,128)}, f32[2,8,48,128]{3,2,1,0:T(8,128)}, f32[2,8,48,128]{3,2,1,0:T(8,128)}) custom-call(s32[2]{0:T(128)} %pad_add_fusion.place_ref, s32[1,12,2]{2,1,0:T(8,128)} %copy.13.off_ref, s32[1,1]{1,0:T(1,128)S(6)} %copy.15.cnt_ref, f32[128,128]{1,0:T(8,128)} %probe_real_ref.1, ...), custom_call_target="tpu_custom_call" | custom-call | tf_op jit(solution)/shard_map/slots/pallas_call | solution.py:222
  67.4 13.7 %collective-permute-start.5 = (f32[2,16,48,128]{3,2,1,0:T(8,128)}, f32[2,16,48,128]{3,2,1,0:T(8,128)S(1)}, u32[]{:S(2)}, u32[]{:S(2)}) collective-permute-start(f32[2,16,48,128]{3,2,1,0:T(8,128)} %get-tuple-element.19), channel_id=1, source_target_pairs={{0,1},{1,0},{2,3},{3,2},{4,5},{5,4},{6,7},{7,6},{8,9},{9,8},{10,11... | collective-permute-start | bytes 2359304 | tf_op jit(solution)/shard_map/reduce/ppermute | solution.py:234
  81.0 1.9 %collective-permute-start.7 = (f32[2,8,48,128]{3,2,1,0:T(8,128)}, f32[2,8,48,128]{3,2,1,0:T(8,128)S(1)}, u32[]{:S(2)}, u32[]{:S(2)}) collective-permute-start(f32[2,8,48,128]{3,2,1,0:T(8,128)} %get-tuple-element.21), channel_id=1, source_target_pairs={{0,1},{1,0},{2,3},{3,2},{4,5},{5,4},{6,7},{7,6},{8,9},{9,8},{10,11... | collective-permute-start | bytes 1179656 | tf_op jit(solution)/shard_map/reduce/ppermute | solution.py:234
  83.0 1.9 %collective-permute-done.7 = f32[2,8,48,128]{3,2,1,0:T(8,128)S(1)} collective-permute-done((f32[2,8,48,128]{3,2,1,0:T(8,128)}, f32[2,8,48,128]{3,2,1,0:T(8,128)S(1)}, u32[]{:S(2)}, u32[]{:S(2)}) %collective-permute-start.7) | collective-permute-done | bytes 393248 | tf_op jit(solution)/shard_map/reduce/ppermute | solution.py:234
  84.9 0.0 copy-start.2
  84.9 1.1 add.21
  86.0 2.3 %collective-permute-start.8 = (f32[8,48,128]{2,1,0:T(8,128)S(1)}, f32[8,48,128]{2,1,0:T(8,128)S(1)}, u32[]{:S(2)}, u32[]{:S(2)}) collective-permute-start(f32[8,48,128]{2,1,0:T(8,128)S(1)} %slice_bitcast_fusion.2), channel_id=1, source_target_pairs={{0,2},{2,0},{1,3},{3,1},{4,6},{6,4},{5,7},{7,5},{8,10},{10,8},{9,1... | collective-permute-start | bytes 589832 | tf_op jit(solution)/shard_map/reduce/ppermute | solution.py:234
  88.3 0.0 collective-permute-done.5
  88.4 0.0 copy-done.2
  88.4 0.1 add.19
  88.5 3.5 %collective-permute-start.6 = (f32[16,48,128]{2,1,0:T(8,128)S(1)}, f32[16,48,128]{2,1,0:T(8,128)S(1)}, u32[]{:S(2)}, u32[]{:S(2)}) collective-permute-start(f32[16,48,128]{2,1,0:T(8,128)S(1)} %slice_bitcast_fusion), channel_id=1, source_target_pairs={{0,2},{2,0},{1,3},{3,1},{4,6},{6,4},{5,7},{7,5},{8,10},{10,8},{9,1... | collective-permute-start | bytes 1179656 | tf_op jit(solution)/shard_map/reduce/ppermute | solution.py:234
  92.0 3.6 %collective-permute-done.8 = f32[8,48,128]{2,1,0:T(8,128)S(1)} collective-permute-done((f32[8,48,128]{2,1,0:T(8,128)S(1)}, f32[8,48,128]{2,1,0:T(8,128)S(1)}, u32[]{:S(2)}, u32[]{:S(2)}) %collective-permute-start.8) | collective-permute-done | bytes 196640 | tf_op jit(solution)/shard_map/reduce/ppermute | solution.py:234
  95.7 1.9 %collective-permute-start.9 = (f32[8,48,128]{2,1,0:T(8,128)S(1)}, f32[8,48,128]{2,1,0:T(8,128)S(1)}, u32[]{:S(2)}, u32[]{:S(2)}) collective-permute-start(f32[8,48,128]{2,1,0:T(8,128)S(1)} %fusion.1), channel_id=1, source_target_pairs={{0,64},{64,128},{128,192},{192,256},{256,320},{320,384},{384,448},... | collective-permute-start | bytes 589832 | tf_op jit(solution)/shard_map/reduce/ppermute | solution.py:239
  97.6 9.9 %collective-permute-done.6 = f32[16,48,128]{2,1,0:T(8,128)S(1)} collective-permute-done((f32[16,48,128]{2,1,0:T(8,128)S(1)}, f32[16,48,128]{2,1,0:T(8,128)S(1)}, u32[]{:S(2)}, u32[]{:S(2)}) %collective-permute-start.6) | collective-permute-done | bytes 393248 | tf_op jit(solution)/shard_map/reduce/ppermute | solution.py:234
  107.5 0.1 fusion
  107.5 0.0 collective-permute-done.9
  107.6 27.5 %all_to_all.11 = f32[16,48,128]{2,1,0:T(8,128)S(1)} all-to-all(f32[16,48,128]{2,1,0:T(8,128)S(1)} %fusion.2), channel_id=1, replica_groups=mesh['region'=8,'z'=16,'yl'=2,'core'=2] {'z'}, dimensions={0} | all-to-all | bytes 786432 | tf_op jit(solution)/shard_map/reduce/all_to_all | solution.py:284
  135.1 0.6 slice_bitcast_fusion.4
  (12 shorter events, 0.3 us)
Async XLA Ops:
  0.6 0.7 copy-start.5
  32.9 16.0 %collective-permute-start = (bf16[16,48,128]{2,1,0:T(8,128)(2,1)S(1)}, bf16[16,48,128]{2,1,0:T(8,128)(2,1)S(1)}, u32[]{:S(2)}, u32[]{:S(2)}) collective-permute-start(bf16[16,48,128]{2,1,0:T(8,128)(2,1)S(1)} %all_to_all.10), channel_id=1, source_target_pairs={{0,2},{2,0},{1,3},{3,1},{4,6},{6,4},{5,7},{7,5},{8,10},{10,8},{9,1... | collective-permute-start | bytes 589832 | tf_op jit(solution)/shard_map/gather/ppermute | solution.py:234
  36.1 10.1 %collective-permute-start.2 = (bf16[8,48,128]{2,1,0:T(8,128)(2,1)S(1)}, bf16[8,48,128]{2,1,0:T(8,128)(2,1)S(1)}, u32[]{:S(2)}, u32[]{:S(2)}) collective-permute-start(bf16[8,48,128]{2,1,0:T(8,128)(2,1)S(1)} %slice.55), channel_id=1, source_target_pairs={{0,448},{64,0},{128,64},{192,128},{256,192},{320,256},{384,320},{4... | collective-permute-start | bytes 294920 | tf_op jit(solution)/shard_map/gather/ppermute | solution.py:239
  46.2 6.5 %collective-permute-start.3 = (bf16[8,48,128]{2,1,0:T(8,128)(2,1)S(1)}, bf16[8,48,128]{2,1,0:T(8,128)(2,1)S(1)}, u32[]{:S(2)}, u32[]{:S(2)}) collective-permute-start(bf16[8,48,128]{2,1,0:T(8,128)(2,1)S(1)} %collective-permute-done.2), channel_id=1, source_target_pairs={{0,2},{2,0},{1,3},{3,1},{4,6},{6,4},{5,7},{7,5},{8,10},{10,8},{9,1... | collective-permute-start | bytes 294920 | tf_op jit(solution)/shard_map/gather/ppermute | solution.py:234
  48.9 7.7 %copy-start = (bf16[2,16,48,128]{3,2,1,0:T(8,128)(2,1)}, bf16[2,16,48,128]{3,2,1,0:T(8,128)(2,1)S(1)}, u32[]{:S(2)}) copy-start(bf16[2,16,48,128]{3,2,1,0:T(8,128)(2,1)S(1)} %pad_maximum_fusion.own_near_ref) | copy-start | bytes 1179652
  48.9 7.7 %collective-permute-start.1 = (bf16[2,16,48,128]{3,2,1,0:T(8,128)(2,1)S(1)}, bf16[2,16,48,128]{3,2,1,0:T(8,128)(2,1)S(1)}, u32[]{:S(2)}, u32[]{:S(2)}) collective-permute-start(bf16[2,16,48,128]{3,2,1,0:T(8,128)(2,1)S(1)} %pad_maximum_fusion.own_near_ref), channel_id=1, source_target_pairs={{0,1},{1,0},{2,3},{3,2},{4,5},{5,4},{6,7},{7,6},{8,9},{9,8},{10,11... | collective-permute-start | bytes 1179656 | tf_op jit(solution)/shard_map/gather/ppermute | solution.py:234
  52.7 3.9 %copy-start.1 = (bf16[2,8,48,128]{3,2,1,0:T(8,128)(2,1)}, bf16[2,8,48,128]{3,2,1,0:T(8,128)(2,1)S(1)}, u32[]{:S(2)}) copy-start(bf16[2,8,48,128]{3,2,1,0:T(8,128)(2,1)S(1)} %pad_maximum_fusion.1.next_near_ref) | copy-start | bytes 589828
  52.7 3.9 %collective-permute-start.4 = (bf16[2,8,48,128]{3,2,1,0:T(8,128)(2,1)S(1)}, bf16[2,8,48,128]{3,2,1,0:T(8,128)(2,1)S(1)}, u32[]{:S(2)}, u32[]{:S(2)}) collective-permute-start(bf16[2,8,48,128]{3,2,1,0:T(8,128)(2,1)S(1)} %pad_maximum_fusion.1.next_near_ref), channel_id=1, source_target_pairs={{0,1},{1,0},{2,3},{3,2},{4,5},{5,4},{6,7},{7,6},{8,9},{9,8},{10,11... | collective-permute-start | bytes 589832 | tf_op jit(solution)/shard_map/gather/ppermute | solution.py:234
  54.7 0.7 copy-start.6
  56.6 0.7 copy-start.4
  56.6 0.8 copy-start.3
  67.4 21.0 %collective-permute-start.5 = (f32[2,16,48,128]{3,2,1,0:T(8,128)}, f32[2,16,48,128]{3,2,1,0:T(8,128)S(1)}, u32[]{:S(2)}, u32[]{:S(2)}) collective-permute-start(f32[2,16,48,128]{3,2,1,0:T(8,128)} %get-tuple-element.19), channel_id=1, source_target_pairs={{0,1},{1,0},{2,3},{3,2},{4,5},{5,4},{6,7},{7,6},{8,9},{9,8},{10,11... | collective-permute-start | bytes 2359304 | tf_op jit(solution)/shard_map/reduce/ppermute | solution.py:234
  81.0 3.8 %collective-permute-start.7 = (f32[2,8,48,128]{3,2,1,0:T(8,128)}, f32[2,8,48,128]{3,2,1,0:T(8,128)S(1)}, u32[]{:S(2)}, u32[]{:S(2)}) collective-permute-start(f32[2,8,48,128]{3,2,1,0:T(8,128)} %get-tuple-element.21), channel_id=1, source_target_pairs={{0,1},{1,0},{2,3},{3,2},{4,5},{5,4},{6,7},{7,6},{8,9},{9,8},{10,11... | collective-permute-start | bytes 1179656 | tf_op jit(solution)/shard_map/reduce/ppermute | solution.py:234
  84.9 3.5 %copy-start.2 = (f32[2,16,48,128]{3,2,1,0:T(8,128)S(1)}, f32[2,16,48,128]{3,2,1,0:T(8,128)}, u32[]{:S(2)}) copy-start(f32[2,16,48,128]{3,2,1,0:T(8,128)} %get-tuple-element.18) | copy-start | bytes 2359300
  86.0 9.6 %collective-permute-start.8 = (f32[8,48,128]{2,1,0:T(8,128)S(1)}, f32[8,48,128]{2,1,0:T(8,128)S(1)}, u32[]{:S(2)}, u32[]{:S(2)}) collective-permute-start(f32[8,48,128]{2,1,0:T(8,128)S(1)} %slice_bitcast_fusion.2), channel_id=1, source_target_pairs={{0,2},{2,0},{1,3},{3,1},{4,6},{6,4},{5,7},{7,5},{8,10},{10,8},{9,1... | collective-permute-start | bytes 589832 | tf_op jit(solution)/shard_map/reduce/ppermute | solution.py:234
  88.5 19.0 %collective-permute-start.6 = (f32[16,48,128]{2,1,0:T(8,128)S(1)}, f32[16,48,128]{2,1,0:T(8,128)S(1)}, u32[]{:S(2)}, u32[]{:S(2)}) collective-permute-start(f32[16,48,128]{2,1,0:T(8,128)S(1)} %slice_bitcast_fusion), channel_id=1, source_target_pairs={{0,2},{2,0},{1,3},{3,1},{4,6},{6,4},{5,7},{7,5},{8,10},{10,8},{9,1... | collective-permute-start | bytes 1179656 | tf_op jit(solution)/shard_map/reduce/ppermute | solution.py:234
  95.7 11.9 %collective-permute-start.9 = (f32[8,48,128]{2,1,0:T(8,128)S(1)}, f32[8,48,128]{2,1,0:T(8,128)S(1)}, u32[]{:S(2)}, u32[]{:S(2)}) collective-permute-start(f32[8,48,128]{2,1,0:T(8,128)S(1)} %fusion.1), channel_id=1, source_target_pairs={{0,64},{64,128},{128,192},{192,256},{256,320},{320,384},{384,448},... | collective-permute-start | bytes 589832 | tf_op jit(solution)/shard_map/reduce/ppermute | solution.py:239

commit v2 on v1

--- a/solution.py
+++ b/solution.py
@@ -93,14 +93,10 @@
     probe_imag_ref,
     pat_ref,
     tab_ref,
-    own_near_ref,
-    own_far_ref,
-    next_near_ref,
-    next_far_ref,
+    near_ref,
+    far_ref,
     keep_ref,
     send_ref,
-    keep_next_ref,
-    send_next_ref,
     obj_ref,
     grad_ref,
 ):
@@ -113,50 +109,40 @@
     grad_ref[...] = jnp.zeros_like(grad_ref)
     top = lax.broadcasted_iota(jnp.int32, (2 * half, w), 0) < half
 
-    def unpack(near_ref, far_ref, first_row):
-        def place(z, _):
-            for y in range(2):
-                row = first_row + (2 * z + lax.rem(y + yl, 2)) * 2 * half
-                row = pl.multiple_of(row, 2 * half)
-                near = near_ref[y, z].astype(jnp.float32)
-                far = far_ref[y, z].astype(jnp.float32)
-                low = jnp.where(first_core, near, far)
-                high = jnp.where(first_core, far, near)
-                for s in range(slices):
-                    for h in range(2):
-                        k = (s * 2 + h) * 2 * half
-                        a, b = low[k : k + 2 * half], high[k : k + 2 * half]
-                        obj_ref[0, s, h, pl.ds(row, 2 * half), :] = jnp.where(
-                            top, a, pltpu.roll(b, half, 0)
-                        )
-                        obj_ref[1, s, h, pl.ds(row, 2 * half), :] = jnp.where(
-                            top, pltpu.roll(a, half, 0), b
-                        )
-            return 0
-
-        lax.fori_loop(0, near_ref.shape[1], place, 0)
-
-    def pack(keep_out, send_out, first_row):
-        def place(z, _):
-            for y in range(2):
-                row = first_row + (2 * z + lax.rem(y + yl, 2)) * 2 * half
-                row = pl.multiple_of(row, 2 * half)
-                for s in range(slices):
-                    for h in range(2):
-                        k = (s * 2 + h) * 2 * half
-                        real = grad_ref[0, s, h, pl.ds(row, 2 * half), :]
-                        imag = grad_ref[1, s, h, pl.ds(row, 2 * half), :]
-                        low = jnp.where(top, real, pltpu.roll(imag, half, 0))
-                        high = jnp.where(top, pltpu.roll(real, half, 0), imag)
-                        keep_out[y, z, k : k + 2 * half] = jnp.where(first_core, low, high)
-                        send_out[y, z, k : k + 2 * half] = jnp.where(first_core, high, low)
-            return 0
-
-        lax.fori_loop(0, keep_out.shape[1], place, 0)
-
-    band_rows = own_near_ref.shape[1] * 4 * half
-    unpack(own_near_ref, own_far_ref, 0)
-    unpack(next_near_ref, next_far_ref, band_rows)
+    def eight_rows(y, z):
+        return pl.ds(pl.multiple_of((2 * z + lax.rem(y + yl, 2)) * 2 * half, 2 * half), 2 * half)
+
+    def unpack(z, _):
+        for y in range(2):
+            rows = eight_rows(y, z)
+            near = near_ref[y, z].astype(jnp.float32)
+            far = far_ref[y, z].astype(jnp.float32)
+            low = jnp.where(first_core, near, far)
+            high = jnp.where(first_core, far, near)
+            for s in range(slices):
+                for h in range(2):
+                    k = (s * 2 + h) * 2 * half
+                    a, b = low[k : k + 2 * half], high[k : k + 2 * half]
+                    obj_ref[0, s, h, rows, :] = jnp.where(top, a, pltpu.roll(b, half, 0))
+                    obj_ref[1, s, h, rows, :] = jnp.where(top, pltpu.roll(a, half, 0), b)
+        return 0
+
+    def pack(z, _):
+        for y in range(2):
+            rows = eight_rows(y, z)
+            for s in range(slices):
+                for h in range(2):
+                    k = (s * 2 + h) * 2 * half
+                    real = grad_ref[0, s, h, rows, :]
+                    imag = grad_ref[1, s, h, rows, :]
+                    low = jnp.where(top, real, pltpu.roll(imag, half, 0))
+                    high = jnp.where(top, pltpu.roll(real, half, 0), imag)
+                    keep_ref[y, z, k : k + 2 * half] = jnp.where(first_core, low, high)
+                    send_ref[y, z, k : k + 2 * half] = jnp.where(first_core, high, low)
+        return 0
+
+    blocks = near_ref.shape[1]
+    lax.fori_loop(0, blocks, unpack, 0)
 
     count = cnt_ref[0, 0]
     lane = lax.broadcasted_iota(jnp.int32, (w, w), 1)
@@ -207,27 +193,24 @@
         return 0
 
     lax.fori_loop(0, lax.div(count + (GROUP - 1), GROUP), visit, 0)
-    pack(keep_next_ref, send_next_ref, band_rows)
-    pack(keep_ref, send_ref, 0)
-
-
-def slots_call(scale, place, offsets, counts, probe, patterns, tables, own, following):
+    lax.fori_loop(0, blocks, pack, 0)
+
+
+def slots_call(scale, place, offsets, counts, probe, patterns, tables, near, far):
     slices = 3
     width = probe[0].shape[0]
-    rows = (own[0].shape[1] + following[0].shape[1]) * 16
     vector = pl.BlockSpec(memory_space=pltpu.VMEM)
     scalar = pl.BlockSpec(memory_space=pltpu.SMEM)
-    held = pltpu.VMEM((2, slices, 2, rows, width), jnp.float32)
-    outs = [jax.ShapeDtypeStruct(x.shape, jnp.float32) for x in (own[0],) * 2 + (following[0],) * 2]
+    held = pltpu.VMEM((2, slices, 2, near.shape[1] * 16, width), jnp.float32)
     return pl.pallas_call(
         functools.partial(slots_kernel, scale),
-        out_shape=outs,
-        in_specs=[scalar] * 3 + [vector] * 8,
-        out_specs=[vector] * 4,
+        out_shape=[jax.ShapeDtypeStruct(near.shape, jnp.float32)] * 2,
+        in_specs=[scalar] * 3 + [vector] * 6,
+        out_specs=[vector] * 2,
         scratch_shapes=[held, held],
-        compiler_params=pltpu.CompilerParams(vmem_limit_bytes=56 * 1024 * 1024),
+        compiler_params=pltpu.CompilerParams(vmem_limit_bytes=40 * 1024 * 1024),
         name="slots",
-    )(place, offsets, counts, *probe, patterns, tables, *own, *following)
+    )(place, offsets, counts, *probe, patterns, tables, near, far)
 
 
 def swap(block, axis):
@@ -237,6 +220,25 @@
 def shift(block, distance):
     bands = lax.axis_size("region")
     return lax.ppermute(block, "region", [(i, (i + distance) % bands) for i in range(bands)])
+
+
+def shift_and_swap(block, distance):
+    bands = lax.axis_size("region")
+    route = [(2 * i + y, (i + distance) % bands * 2 + 1 - y) for i in range(bands) for y in (0, 1)]
+    return lax.ppermute(block, ("region", "yl"), route)
+
+
+def encode(blocks, over):
+    most = jnp.max(jnp.abs(blocks), axis=over, keepdims=True)
+    code = jnp.ceil(jnp.log2(jnp.maximum(most, 1e-37)) * 64.0)
+    share = jnp.clip(jnp.round(blocks * jnp.exp2(code / -64.0) * 32767.0), -32767.0, 32767.0)
+    return share.astype(jnp.int16), code[0].astype(jnp.int16)
+
+
+def decode(message, axis):
+    code = lax.slice_in_dim(message, message.shape[axis] - 1, None, axis=axis)
+    share = lax.slice_in_dim(message, 0, message.shape[axis] - 1, axis=axis)
+    return share.astype(jnp.float32) * (jnp.exp2(code.astype(jnp.float32) / 64.0) / 32767.0)
 
 
 def local(tables, object_real, object_imag, probe_real, probe_imag, patterns, offsets, counts):
@@ -244,44 +246,47 @@
     width = probe_real.shape[0]
     halves = columns // width
     depth = lax.axis_size("z")
-    below = depth * width // (depth * 4 * rows)
+    below = width // (4 * rows)
     packed = slices * halves * 2 * rows
-    yl = lax.axis_index("yl")
-    place = jnp.stack([yl, lax.axis_index("core")]).astype(jnp.int32)
+    place = jnp.stack([lax.axis_index("yl"), lax.axis_index("core")]).astype(jnp.int32)
     scale = 1.0 / math.sqrt(patterns.shape[1] * depth * 4)
 
     with jax.named_scope("gather"):
         block = jnp.stack([object_real, object_imag]).reshape(2, slices, rows, halves, width)
-        block = block.transpose(1, 3, 0, 2, 4).reshape(1, packed, width)
+        block = block.transpose(1, 3, 0, 2, 4).reshape(packed, width)
         column = lax.all_to_all(
             jnp.broadcast_to(block, (depth, packed, width)), "z", 0, 0, tiled=True
         )
+        other = swap(column, "yl")
         following = shift(column[:below], -1)
-        other = swap(column, "yl")
-        own = jnp.stack([column, other])
-        own_far = swap(own, "core")
-        following = jnp.stack([following, swap(following, "yl")])
-        following_far = swap(following, "core")
-
-    keep, send, keep_next, send_next = slots_call(
-        scale,
-        place,
-        offsets,
-        counts,
-        (probe_real, probe_imag),
-        patterns[0],
-        tables,
-        (own, own_far),
-        (following, following_far),
+        following_other = shift_and_swap(column[:below], -1)
+        near = jnp.concatenate([column, following, other, following_other])
+        near = near.reshape(2, depth + below, packed, width)
+        far = swap(near, "core")
+
+    keep, send = slots_call(
+        scale, place, offsets, counts, (probe_real, probe_imag), patterns[0], tables, near, far
     )
 
     with jax.named_scope("reduce"):
-        carried = keep_next + swap(send_next, "core")
         total = keep + swap(send, "core")
-        carried = carried[0] + swap(carried[1], "yl")
-        total = total[0] + swap(total[1], "yl")
-        total = total.at[:below].add(shift(carried, 1))
-        total = lax.all_to_all(total, "z", 0, 0, tiled=True).sum(0)
+        away = jnp.concatenate([total[1], total[0, depth:]])
+        share, code = encode(away, (0,))
+        code = code[None]
+        near_next = jnp.concatenate([share[depth + below :], code])
+        far_next = jnp.concatenate([share[depth : depth + below], code])
+        beside = jnp.concatenate([share[:depth], code])
+        far_next = shift_and_swap(far_next, 1)
+        near_next = shift(near_next, 1)
+        beside = swap(beside, "yl")
+        total = total[0, :depth] + decode(beside, 0)
+        total = total.at[:below].add(decode(near_next, 0) + decode(far_next, 0))
+        total = total.reshape(depth, -1, 2 * rows, width)
+        share, code = encode(total, (0, 1))
+        code = jnp.broadcast_to(code, (depth,) + code.shape)
+        message = jnp.concatenate([share, code], axis=1).reshape(depth, -1, width)
+        message = lax.all_to_all(message, "z", 0, 0, tiled=True)
+        total = decode(message.reshape(depth, -1, 2 * rows, width), 1).sum(0)
         total = total.reshape(slices, halves, 2, rows, width).transpose(2, 0, 3, 1, 4)
         total = total.reshape(2, slices, rows, columns)
     return total[0], total[1]

time: 136 us -> 117 us (0.86)
  the two profiles are of different devices: /device:TPU:22 before, /device:TPU:6 now
where the time goes in v2:
time: 117 us
  blocking collectives  55.1 us (47%)
  starting transfers between devices  34.3 us (29%)
  waiting for transfers between devices  15.8 us (14%)
  Pallas kernels  7.45 us (6%)
  other arithmetic  1.87 us (2%)
  between operations  1.6 us (1%)
    all_to_all x1, blocking collectives, local(): lax.all_to_all(jnp.broadcast_to(block, (depth, packed, width)), 'z', 0, 0...  31.4 us
    all_to_all x1, blocking collectives, local(): message = lax.all_to_all(message, 'z', 0, 0, tiled=True)  23.6 us
    ppermute x4, starting transfers between devices, swap(): return lax.ppermute(block, axis, [(0, 1), (1, 0)])  15 us
    ppermute x2, starting transfers between devices, shift(): lax.ppermute(block, 'region', [(i, (i + distance) % bands) for i in range...  13 us
    pallas_call x1, Pallas kernels, slots_call(): pl.pallas_call(functools.partial(slots_kernel, scale), out_shape=[jax.Sha...  7.45 us
    ppermute x2, starting transfers between devices, shift_and_swap(): return lax.ppermute(block, ('region', 'yl'), route)  6.28 us
    ppermute x2, waiting for transfers between devices, shift_and_swap(): return lax.ppermute(block, ('region', 'yl'), route)  6.08 us
    ppermute x4, waiting for transfers between devices, swap(): return lax.ppermute(block, axis, [(0, 1), (1, 0)])  5.52 us
  transfers between devices with their start and end apart: 8, of which 6 were waited for; matrix products, arithmetic and copies ran while one was open for 0% of the time, Pallas kernels for 0%

profile of v2, /device:TPU:6, one launch (start us, length us, event | category | flops | bytes accessed | tf_op | source)
XLA Modules:
  0.0 116.9 jit_solution(2506646851813875349)
XLA Ops:
  0.6 0.0 copy-start
  0.6 0.0 copy-start.4
  0.7 0.0 copy-start.1
  0.7 0.0 copy-start.3
  0.7 0.0 copy-start.2
  0.7 0.8 pad_maximum_fusion.2
  1.6 31.4 %all_to_all.10 = bf16[16,48,128]{2,1,0:T(8,128)(2,1)S(1)} all-to-all(bf16[16,48,128]{2,1,0:T(8,128)(2,1)S(1)} %broadcast_in_dim.4), channel_id=1, replica_groups=mesh['region'=8,'z'=16,'yl'=2,'core'=2] {'z'}, dimensions={0} | all-to-all | bytes 393216 | tf_op jit(solution)/shard_map/gather/all_to_all | solution.py:257
  33.0 3.5 %collective-permute-start.1 = (bf16[16,48,128]{2,1,0:T(8,128)(2,1)S(1)}, bf16[16,48,128]{2,1,0:T(8,128)(2,1)S(1)}, u32[]{:S(2)}, u32[]{:S(2)}) collective-permute-start(bf16[16,48,128]{2,1,0:T(8,128)(2,1)S(1)} %all_to_all.10), channel_id=1, source_target_pairs={{0,2},{2,0},{1,3},{3,1},{4,6},{6,4},{5,7},{7,5},{8,10},{10,8},{9,1... | collective-permute-start | bytes 589832 | tf_op jit(solution)/shard_map/gather/ppermute | solution.py:217
  36.5 4.4 %collective-permute-start.2 = (bf16[8,48,128]{2,1,0:T(8,128)(2,1)S(1)}, bf16[8,48,128]{2,1,0:T(8,128)(2,1)S(1)}, u32[]{:S(2)}, u32[]{:S(2)}) collective-permute-start(bf16[8,48,128]{2,1,0:T(8,128)(2,1)S(1)} %slice.96), channel_id=1, source_target_pairs={{0,450},{2,448},{64,2},{66,0},{128,66},{130,64},{192,130},{194,128... | collective-permute-start | bytes 294920 | tf_op jit(solution)/shard_map/gather/ppermute | solution.py:228
  40.8 2.6 %collective-permute-start = (bf16[8,48,128]{2,1,0:T(8,128)(2,1)S(1)}, bf16[8,48,128]{2,1,0:T(8,128)(2,1)S(1)}, u32[]{:S(2)}, u32[]{:S(2)}) collective-permute-start(bf16[8,48,128]{2,1,0:T(8,128)(2,1)S(1)} %slice.96), channel_id=1, source_target_pairs={{0,448},{64,0},{128,64},{192,128},{256,192},{320,256},{384,320},{4... | collective-permute-start | bytes 294920 | tf_op jit(solution)/shard_map/gather/ppermute | solution.py:222
  43.5 1.2 collective-permute-done.2
  44.7 4.2 %collective-permute-done = bf16[8,48,128]{2,1,0:T(8,128)(2,1)S(1)} collective-permute-done((bf16[8,48,128]{2,1,0:T(8,128)(2,1)S(1)}, bf16[8,48,128]{2,1,0:T(8,128)(2,1)S(1)}, u32[]{:S(2)}, u32[]{:S(2)}) %collective-permute-start) | collective-permute-done | bytes 98336 | tf_op jit(solution)/shard_map/gather/ppermute | solution.py:222
  48.9 0.0 collective-permute-done.1
  48.9 0.1 pad_maximum_fusion.1
  48.9 1.9 %collective-permute-start.3 = (bf16[2,24,48,128]{3,2,1,0:T(8,128)(2,1)S(1)}, bf16[2,24,48,128]{3,2,1,0:T(8,128)(2,1)S(1)}, u32[]{:S(2)}, u32[]{:S(2)}) collective-permute-start(bf16[2,24,48,128]{3,2,1,0:T(8,128)(2,1)S(1)} %bitcast.49), channel_id=1, source_target_pairs={{0,1},{1,0},{2,3},{3,2},{4,5},{5,4},{6,7},{7,6},{8,9},{9,8},{10,11... | collective-permute-start | bytes 1769480 | tf_op jit(solution)/shard_map/gather/ppermute | solution.py:217
  51.5 0.0 copy-done.4
  51.5 0.1 copy.16.off_ref
  51.6 0.1 pad_add_fusion.3.place_ref
  51.7 1.1 collective-permute-done.3.far_ref
  52.8 0.0 copy-done
  52.8 0.0 copy-done.1
  52.8 0.0 copy-done.3
  52.9 0.0 copy-done.2
  52.9 7.4 %slots.1 = (f32[2,24,48,128]{3,2,1,0:T(8,128)S(1)}, f32[2,24,48,128]{3,2,1,0:T(8,128)S(1)}) custom-call(s32[2]{0:T(128)S(1)} %pad_add_fusion.3.place_ref, s32[1,12,2]{2,1,0:T(8,128)S(1)} %copy.16.off_ref, s32[1,1]{1,0:T(1,128)S(6)} %copy.18.cnt_ref, f32[128,128]{1,0:T(8,128)S(1)} %copy-done.2, f32[128,128]{1,0:T(8,128)S(1)} %copy-done.3, ...), custom_call_target="tpu_custom_call" | custom-call | tf_op jit(solution)/shard_map/slots/pallas_call | solution.py:205
  60.3 7.7 %collective-permute-start.4 = (f32[2,24,48,128]{3,2,1,0:T(8,128)S(1)}, f32[2,24,48,128]{3,2,1,0:T(8,128)S(1)}, u32[]{:S(2)}, u32[]{:S(2)}) collective-permute-start(f32[2,24,48,128]{3,2,1,0:T(8,128)S(1)} %get-tuple-element.17), channel_id=1, source_target_pairs={{0,1},{1,0},{2,3},{3,2},{4,5},{5,4},{6,7},{7,6},{8,9},{9,8},{10,11... | collective-permute-start | bytes 3538952 | tf_op jit(solution)/shard_map/reduce/ppermute | solution.py:217
  68.0 2.5 %collective-permute-done.4 = f32[2,24,48,128]{3,2,1,0:T(8,128)S(1)} collective-permute-done((f32[2,24,48,128]{3,2,1,0:T(8,128)S(1)}, f32[2,24,48,128]{3,2,1,0:T(8,128)S(1)}, u32[]{:S(2)}, u32[]{:S(2)}) %collective-permute-start.4) | collective-permute-done | bytes 1179680 | tf_op jit(solution)/shard_map/reduce/ppermute | solution.py:217
  70.4 0.1 add.16
  70.7 0.1 clamp_convert_fusion
  70.9 10.4 %collective-permute-start.6 = (s16[9,48,128]{2,1,0:T(8,128)(2,1)S(1)}, s16[9,48,128]{2,1,0:T(8,128)(2,1)S(1)}, u32[]{:S(2)}, u32[]{:S(2)}) collective-permute-start(s16[9,48,128]{2,1,0:T(8,128)(2,1)S(1)} %get-tuple-element.24), channel_id=1, source_target_pairs={{0,64},{64,128},{128,192},{192,256},{256,320},{320,384},{384,448},... | collective-permute-start | bytes 331784 | tf_op jit(solution)/shard_map/reduce/ppermute | solution.py:222
  81.3 1.9 %collective-permute-start.7 = (s16[9,48,128]{2,1,0:T(8,128)(2,1)S(1)}, s16[9,48,128]{2,1,0:T(8,128)(2,1)S(1)}, u32[]{:S(2)}, u32[]{:S(2)}) collective-permute-start(s16[9,48,128]{2,1,0:T(8,128)(2,1)S(1)} %get-tuple-element.25), channel_id=1, source_target_pairs={{0,66},{2,64},{64,130},{66,128},{128,194},{130,192},{192,258},{194... | collective-permute-start | bytes 331784 | tf_op jit(solution)/shard_map/reduce/ppermute | solution.py:228
  83.3 1.9 %collective-permute-start.5 = (s16[17,48,128]{2,1,0:T(8,128)(2,1)S(1)}, s16[17,48,128]{2,1,0:T(8,128)(2,1)S(1)}, u32[]{:S(2)}, u32[]{:S(2)}) collective-permute-start(s16[17,48,128]{2,1,0:T(8,128)(2,1)S(1)} %pad_add_fusion), channel_id=1, source_target_pairs={{0,2},{2,0},{1,3},{3,1},{4,6},{6,4},{5,7},{7,5},{8,10},{10,8},{9,1... | collective-permute-start | bytes 626696 | tf_op jit(solution)/shard_map/reduce/ppermute | solution.py:217
  85.2 0.0 collective-permute-done.6
  85.2 4.9 %collective-permute-done.7 = s16[9,48,128]{2,1,0:T(8,128)(2,1)S(1)} collective-permute-done((s16[9,48,128]{2,1,0:T(8,128)(2,1)S(1)}, s16[9,48,128]{2,1,0:T(8,128)(2,1)S(1)}, u32[]{:S(2)}, u32[]{:S(2)}) %collective-permute-start.7) | collective-permute-done | bytes 110624 | tf_op jit(solution)/shard_map/reduce/ppermute | solution.py:228
  90.2 1.9 %collective-permute-done.5 = s16[17,48,128]{2,1,0:T(8,128)(2,1)S(1)} collective-permute-done((s16[17,48,128]{2,1,0:T(8,128)(2,1)S(1)}, s16[17,48,128]{2,1,0:T(8,128)(2,1)S(1)}, u32[]{:S(2)}, u32[]{:S(2)}) %collective-permute-start.5) | collective-permute-done | bytes 208928 | tf_op jit(solution)/shard_map/reduce/ppermute | solution.py:217
  92.1 0.1 fusion
  92.2 0.1 fusion.5
  92.4 0.1 fusion.4
  92.5 23.6 %all_to_all.11 = s16[16,56,128]{2,1,0:T(8,128)(2,1)S(1)} all-to-all(s16[16,56,128]{2,1,0:T(8,128)(2,1)S(1)} %add_bitcast_fusion), channel_id=1, replica_groups=mesh['region'=8,'z'=16,'yl'=2,'core'=2] {'z'}, dimensions={0} | all-to-all | bytes 458752 | tf_op jit(solution)/shard_map/reduce/all_to_all | solution.py:288
  116.2 0.1 multiply_reduce_fusion
  116.3 0.6 slice_bitcast_fusion.3
  (19 shorter events, 0.4 us)
Async XLA Ops:
  0.6 52.2 %copy-start = (bf16[4,2,256,256]{3,2,1,0:T(8,128)(2,1)S(1)}, bf16[4,2,256,256]{3,2,1,0:T(8,128)(2,1)}, u32[]{:S(2)}) copy-start(bf16[4,2,256,256]{3,2,1,0:T(8,128)(2,1)} %constant.82.clone.tab_ref) | copy-start | bytes 3145732
  0.6 50.9 %copy-start.4 = (s32[1,12,2]{1,2,0:T(2,128)S(1)}, s32[1,12,2]{1,2,0:T(2,128)}, u32[]{:S(2)}) copy-start(s32[1,12,2]{1,2,0:T(2,128)} %param.15) | copy-start | bytes 292
  0.7 52.2 %copy-start.1 = (bf16[1,12,128,128]{3,2,1,0:T(8,128)(2,1)S(1)}, bf16[1,12,128,128]{3,2,1,0:T(8,128)(2,1)}, u32[]{:S(2)}) copy-start(bf16[1,12,128,128]{3,2,1,0:T(8,128)(2,1)} %param.14) | copy-start | bytes 1179652
  0.7 52.2 %copy-start.3 = (f32[128,128]{1,0:T(8,128)S(1)}, f32[128,128]{1,0:T(8,128)}, u32[]{:S(2)}) copy-start(f32[128,128]{1,0:T(8,128)} %probe_imag_ref.1) | copy-start | bytes 196612
  0.7 52.2 %copy-start.2 = (f32[128,128]{1,0:T(8,128)S(1)}, f32[128,128]{1,0:T(8,128)}, u32[]{:S(2)}) copy-start(f32[128,128]{1,0:T(8,128)} %probe_real_ref.1) | copy-start | bytes 196612
  33.0 15.9 %collective-permute-start.1 = (bf16[16,48,128]{2,1,0:T(8,128)(2,1)S(1)}, bf16[16,48,128]{2,1,0:T(8,128)(2,1)S(1)}, u32[]{:S(2)}, u32[]{:S(2)}) collective-permute-start(bf16[16,48,128]{2,1,0:T(8,128)(2,1)S(1)} %all_to_all.10), channel_id=1, source_target_pairs={{0,2},{2,0},{1,3},{3,1},{4,6},{6,4},{5,7},{7,5},{8,10},{10,8},{9,1... | collective-permute-start | bytes 589832 | tf_op jit(solution)/shard_map/gather/ppermute | solution.py:217
  36.5 8.2 %collective-permute-start.2 = (bf16[8,48,128]{2,1,0:T(8,128)(2,1)S(1)}, bf16[8,48,128]{2,1,0:T(8,128)(2,1)S(1)}, u32[]{:S(2)}, u32[]{:S(2)}) collective-permute-start(bf16[8,48,128]{2,1,0:T(8,128)(2,1)S(1)} %slice.96), channel_id=1, source_target_pairs={{0,450},{2,448},{64,2},{66,0},{128,66},{130,64},{192,130},{194,128... | collective-permute-start | bytes 294920 | tf_op jit(solution)/shard_map/gather/ppermute | solution.py:228
  40.8 8.0 %collective-permute-start = (bf16[8,48,128]{2,1,0:T(8,128)(2,1)S(1)}, bf16[8,48,128]{2,1,0:T(8,128)(2,1)S(1)}, u32[]{:S(2)}, u32[]{:S(2)}) collective-permute-start(bf16[8,48,128]{2,1,0:T(8,128)(2,1)S(1)} %slice.96), channel_id=1, source_target_pairs={{0,448},{64,0},{128,64},{192,128},{256,192},{320,256},{384,320},{4... | collective-permute-start | bytes 294920 | tf_op jit(solution)/shard_map/gather/ppermute | solution.py:222
  48.9 3.9 %collective-permute-start.3 = (bf16[2,24,48,128]{3,2,1,0:T(8,128)(2,1)S(1)}, bf16[2,24,48,128]{3,2,1,0:T(8,128)(2,1)S(1)}, u32[]{:S(2)}, u32[]{:S(2)}) collective-permute-start(bf16[2,24,48,128]{3,2,1,0:T(8,128)(2,1)S(1)} %bitcast.49), channel_id=1, source_target_pairs={{0,1},{1,0},{2,3},{3,2},{4,5},{5,4},{6,7},{7,6},{8,9},{9,8},{10,11... | collective-permute-start | bytes 1769480 | tf_op jit(solution)/shard_map/gather/ppermute | solution.py:217
  60.3 10.1 %collective-permute-start.4 = (f32[2,24,48,128]{3,2,1,0:T(8,128)S(1)}, f32[2,24,48,128]{3,2,1,0:T(8,128)S(1)}, u32[]{:S(2)}, u32[]{:S(2)}) collective-permute-start(f32[2,24,48,128]{3,2,1,0:T(8,128)S(1)} %get-tuple-element.17), channel_id=1, source_target_pairs={{0,1},{1,0},{2,3},{3,2},{4,5},{5,4},{6,7},{7,6},{8,9},{9,8},{10,11... | collective-permute-start | bytes 3538952 | tf_op jit(solution)/shard_map/reduce/ppermute | solution.py:217
  70.9 14.3 %collective-permute-start.6 = (s16[9,48,128]{2,1,0:T(8,128)(2,1)S(1)}, s16[9,48,128]{2,1,0:T(8,128)(2,1)S(1)}, u32[]{:S(2)}, u32[]{:S(2)}) collective-permute-start(s16[9,48,128]{2,1,0:T(8,128)(2,1)S(1)} %get-tuple-element.24), channel_id=1, source_target_pairs={{0,64},{64,128},{128,192},{192,256},{256,320},{320,384},{384,448},... | collective-permute-start | bytes 331784 | tf_op jit(solution)/shard_map/reduce/ppermute | solution.py:222
  81.3 8.8 %collective-permute-start.7 = (s16[9,48,128]{2,1,0:T(8,128)(2,1)S(1)}, s16[9,48,128]{2,1,0:T(8,128)(2,1)S(1)}, u32[]{:S(2)}, u32[]{:S(2)}) collective-permute-start(s16[9,48,128]{2,1,0:T(8,128)(2,1)S(1)} %get-tuple-element.25), channel_id=1, source_target_pairs={{0,66},{2,64},{64,130},{66,128},{128,194},{130,192},{192,258},{194... | collective-permute-start | bytes 331784 | tf_op jit(solution)/shard_map/reduce/ppermute | solution.py:228
  83.3 8.8 %collective-permute-start.5 = (s16[17,48,128]{2,1,0:T(8,128)(2,1)S(1)}, s16[17,48,128]{2,1,0:T(8,128)(2,1)S(1)}, u32[]{:S(2)}, u32[]{:S(2)}) collective-permute-start(s16[17,48,128]{2,1,0:T(8,128)(2,1)S(1)} %pad_add_fusion), channel_id=1, source_target_pairs={{0,2},{2,0},{1,3},{3,1},{4,6},{6,4},{5,7},{7,5},{8,10},{10,8},{9,1... | collective-permute-start | bytes 626696 | tf_op jit(solution)/shard_map/reduce/ppermute | solution.py:217

commit v3 on v2

--- a/solution.py
+++ b/solution.py
@@ -11,7 +11,7 @@
 from jax.sharding import PartitionSpec as P
 
 FRESNEL = 12.0
-GROUP = 4
+GROUP = 6
 PROP, DFT = 0, 2
 POS = ("z", "yl", "core")
 
@@ -43,6 +43,15 @@
     return jnp.dot(first, second, preferred_element_type=jnp.float32)
 
 
+def pairs(product, table_ref, which, real, imag):
+    out_real, out_imag = [], []
+    for k in range(0, len(real), 2):
+        found = product(table_ref, which, real[k : k + 2], imag[k : k + 2])
+        out_real += found[0]
+        out_imag += found[1]
+    return out_real, out_imag
+
+
 def left(table_ref, which, real, imag):
     field = jnp.concatenate(
         [jnp.concatenate(real, axis=1), jnp.concatenate(imag, axis=1)], axis=0
@@ -69,7 +78,8 @@
 
 def transform(table_ref, base, adjoint, field):
     flip = 1 if adjoint else 0
-    return right(table_ref, base + flip, *left(table_ref, base + 1 - flip, *field))
+    field = pairs(left, table_ref, base + 1 - flip, *field)
+    return pairs(right, table_ref, base + flip, *field)
 
 
 def mul(first, second):
@@ -208,7 +218,7 @@
         in_specs=[scalar] * 3 + [vector] * 6,
         out_specs=[vector] * 2,
         scratch_shapes=[held, held],
-        compiler_params=pltpu.CompilerParams(vmem_limit_bytes=40 * 1024 * 1024),
+        compiler_params=pltpu.CompilerParams(vmem_limit_bytes=44 * 1024 * 1024),
         name="slots",
     )(place, offsets, counts, *probe, patterns, tables, near, far)
 
@@ -258,8 +268,8 @@
             jnp.broadcast_to(block, (depth, packed, width)), "z", 0, 0, tiled=True
         )
         other = swap(column, "yl")
-        following = shift(column[:below], -1)
         following_other = shift_and_swap(column[:below], -1)
+        following = swap(following_other, "yl")
         near = jnp.concatenate([column, following, other, following_other])
         near = near.reshape(2, depth + below, packed, width)
         far = swap(near, "core")

time: 117 us -> 112 us (0.957)
  starting transfers between devices: 34.3 us -> 24.3 us
  Pallas kernels: 7.45 us -> 11.4 us
  waiting for transfers between devices: 15.8 us -> 18.1 us
  blocking collectives: 55.1 us -> 53 us
    ppermute x2 -> x1, starting transfers between devices: 13 us -> 5.7 us  [shift(): lax.ppermute(block, 'region', [(i, (i + distance) % bands) for i in range...]
    ppermute x4 -> x5, waiting for transfers between devices: 5.52 us -> 11 us  [swap(): return lax.ppermute(block, axis, [(0, 1), (1, 0)])]
    ppermute x2 -> x1, waiting for transfers between devices: 4.2 us -> 0.01 us  [shift(): lax.ppermute(block, 'region', [(i, (i + distance) % bands) for i in range...]
    pallas_call x1, Pallas kernels: 7.45 us -> 11.4 us  [slots_call(): pl.pallas_call(functools.partial(slots_kernel, scale), out_shape=[jax.Sha...]
    ppermute x4 -> x5, starting transfers between devices: 15 us -> 12 us  [swap(): return lax.ppermute(block, axis, [(0, 1), (1, 0)])]
    all_to_all x1, blocking collectives: 23.6 us -> 21.6 us  [local(): message = lax.all_to_all(message, 'z', 0, 0, tiled=True)]
where the time goes in v3:
time: 112 us; the launch traced here: 111 us
  blocking collectives  53 us (47%)
  starting transfers between devices  24.3 us (22%)
  waiting for transfers between devices  18.1 us (16%)
  Pallas kernels  11.4 us (10%)
  other arithmetic  1.87 us (2%)
  between operations  1.6 us (1%)
    all_to_all x1, blocking collectives, local(): lax.all_to_all(jnp.broadcast_to(block, (depth, packed, width)), 'z', 0, 0...  31.4 us
    all_to_all x1, blocking collectives, local(): message = lax.all_to_all(message, 'z', 0, 0, tiled=True)  21.6 us
    ppermute x5, starting transfers between devices, swap(): return lax.ppermute(block, axis, [(0, 1), (1, 0)])  12 us
    pallas_call x1, Pallas kernels, slots_call(): pl.pallas_call(functools.partial(slots_kernel, scale), out_shape=[jax.Sha...  11.4 us
    ppermute x5, waiting for transfers between devices, swap(): return lax.ppermute(block, axis, [(0, 1), (1, 0)])  11 us
    ppermute x2, waiting for transfers between devices, shift_and_swap(): return lax.ppermute(block, ('region', 'yl'), route)  7.11 us
    ppermute x2, starting transfers between devices, shift_and_swap(): return lax.ppermute(block, ('region', 'yl'), route)  6.59 us
    ppermute x1, starting transfers between devices, shift(): lax.ppermute(block, 'region', [(i, (i + distance) % bands) for i in range...  5.7 us
  transfers between devices with their start and end apart: 8, of which 6 were waited for; matrix products, arithmetic and copies ran while one was open for 0% of the time, Pallas kernels for 0%

profile of v3, /device:TPU:6, one launch (start us, length us, event | category | flops | bytes accessed | tf_op | source)
XLA Modules:
  0.0 111.2 jit_solution(8873342884431392424)
XLA Ops:
  0.6 0.0 copy-start
  0.6 0.0 copy-start.4
  0.7 0.0 copy-start.1
  0.7 0.0 copy-start.3
  0.7 0.0 copy-start.2
  0.7 0.8 pad_maximum_fusion.2
  1.6 31.4 %all_to_all.10 = bf16[16,48,128]{2,1,0:T(8,128)(2,1)S(1)} all-to-all(bf16[16,48,128]{2,1,0:T(8,128)(2,1)S(1)} %broadcast_in_dim.4), channel_id=1, replica_groups=mesh['region'=8,'z'=16,'yl'=2,'core'=2] {'z'}, dimensions={0} | all-to-all | bytes 393216 | tf_op jit(solution)/shard_map/gather/all_to_all | solution.py:267
  33.0 3.5 %collective-permute-start.2 = (bf16[16,48,128]{2,1,0:T(8,128)(2,1)S(1)}, bf16[16,48,128]{2,1,0:T(8,128)(2,1)S(1)}, u32[]{:S(2)}, u32[]{:S(2)}) collective-permute-start(bf16[16,48,128]{2,1,0:T(8,128)(2,1)S(1)} %all_to_all.10), channel_id=1, source_target_pairs={{0,2},{2,0},{1,3},{3,1},{4,6},{6,4},{5,7},{7,5},{8,10},{10,8},{9,1... | collective-permute-start | bytes 589832 | tf_op jit(solution)/shard_map/gather/ppermute | solution.py:227
  36.5 4.4 %collective-permute-start = (bf16[8,48,128]{2,1,0:T(8,128)(2,1)S(1)}, bf16[8,48,128]{2,1,0:T(8,128)(2,1)S(1)}, u32[]{:S(2)}, u32[]{:S(2)}) collective-permute-start(bf16[8,48,128]{2,1,0:T(8,128)(2,1)S(1)} %slice.95), channel_id=1, source_target_pairs={{0,450},{2,448},{64,2},{66,0},{128,66},{130,64},{192,130},{194,128... | collective-permute-start | bytes 294920 | tf_op jit(solution)/shard_map/gather/ppermute | solution.py:238
  40.8 3.4 %collective-permute-done = bf16[8,48,128]{2,1,0:T(8,128)(2,1)S(1)} collective-permute-done((bf16[8,48,128]{2,1,0:T(8,128)(2,1)S(1)}, bf16[8,48,128]{2,1,0:T(8,128)(2,1)S(1)}, u32[]{:S(2)}, u32[]{:S(2)}) %collective-permute-start) | collective-permute-done | bytes 98336 | tf_op jit(solution)/shard_map/gather/ppermute | solution.py:238
  44.2 1.9 %collective-permute-start.1 = (bf16[8,48,128]{2,1,0:T(8,128)(2,1)S(1)}, bf16[8,48,128]{2,1,0:T(8,128)(2,1)S(1)}, u32[]{:S(2)}, u32[]{:S(2)}) collective-permute-start(bf16[8,48,128]{2,1,0:T(8,128)(2,1)S(1)} %collective-permute-done), channel_id=1, source_target_pairs={{0,2},{2,0},{1,3},{3,1},{4,6},{6,4},{5,7},{7,5},{8,10},{10,8},{9,1... | collective-permute-start | bytes 294920 | tf_op jit(solution)/shard_map/gather/ppermute | solution.py:227
  46.1 0.0 collective-permute-done.2
  46.1 4.6 %collective-permute-done.1 = bf16[8,48,128]{2,1,0:T(8,128)(2,1)S(1)} collective-permute-done((bf16[8,48,128]{2,1,0:T(8,128)(2,1)S(1)}, bf16[8,48,128]{2,1,0:T(8,128)(2,1)S(1)}, u32[]{:S(2)}, u32[]{:S(2)}) %collective-permute-start.1) | collective-permute-done | bytes 98336 | tf_op jit(solution)/shard_map/gather/ppermute | solution.py:227
  50.7 0.1 pad_maximum_fusion.1
  50.8 1.9 %collective-permute-start.3 = (bf16[2,24,48,128]{3,2,1,0:T(8,128)(2,1)S(1)}, bf16[2,24,48,128]{3,2,1,0:T(8,128)(2,1)S(1)}, u32[]{:S(2)}, u32[]{:S(2)}) collective-permute-start(bf16[2,24,48,128]{3,2,1,0:T(8,128)(2,1)S(1)} %bitcast.49), channel_id=1, source_target_pairs={{0,1},{1,0},{2,3},{3,2},{4,5},{5,4},{6,7},{7,6},{8,9},{9,8},{10,11... | collective-permute-start | bytes 1769480 | tf_op jit(solution)/shard_map/gather/ppermute | solution.py:227
  53.4 0.0 copy-done.4
  53.4 0.1 copy.16.off_ref
  53.5 0.1 pad_add_fusion.3.place_ref
  53.6 1.1 %collective-permute-done.3.far_ref = bf16[2,24,48,128]{3,2,1,0:T(8,128)(2,1)S(1)} collective-permute-done((bf16[2,24,48,128]{3,2,1,0:T(8,128)(2,1)S(1)}, bf16[2,24,48,128]{3,2,1,0:T(8,128)(2,1)S(1)}, u32[]{:S(2)}, u32[]{:S(2)}) %collective-permute-start.3) | collective-permute-done | bytes 589856 | tf_op jit(solution)/shard_map/gather/ppermute | solution.py:227
  54.7 0.0 copy-done
  54.7 0.0 copy-done.1
  54.7 0.0 copy-done.3
  54.7 0.0 copy-done.2
  54.7 11.4 %slots.1 = (f32[2,24,48,128]{3,2,1,0:T(8,128)S(1)}, f32[2,24,48,128]{3,2,1,0:T(8,128)S(1)}) custom-call(s32[2]{0:T(128)S(1)} %pad_add_fusion.3.place_ref, s32[1,12,2]{2,1,0:T(8,128)S(1)} %copy.16.off_ref, s32[1,1]{1,0:T(1,128)S(6)} %copy.18.cnt_ref, f32[128,128]{1,0:T(8,128)S(1)} %copy-done.2, f32[128,128]{1,0:T(8,128)S(1)} %copy-done.3, ...), custom_call_target="tpu_custom_call" | custom-call | tf_op jit(solution)/shard_map/slots/pallas_call | solution.py:215
  66.2 1.9 %collective-permute-start.4 = (f32[2,24,48,128]{3,2,1,0:T(8,128)S(1)}, f32[2,24,48,128]{3,2,1,0:T(8,128)S(1)}, u32[]{:S(2)}, u32[]{:S(2)}) collective-permute-start(f32[2,24,48,128]{3,2,1,0:T(8,128)S(1)} %get-tuple-element.17), channel_id=1, source_target_pairs={{0,1},{1,0},{2,3},{3,2},{4,5},{5,4},{6,7},{7,6},{8,9},{9,8},{10,11... | collective-permute-start | bytes 3538952 | tf_op jit(solution)/shard_map/reduce/ppermute | solution.py:227
  68.1 2.8 %collective-permute-done.4 = f32[2,24,48,128]{3,2,1,0:T(8,128)S(1)} collective-permute-done((f32[2,24,48,128]{3,2,1,0:T(8,128)S(1)}, f32[2,24,48,128]{3,2,1,0:T(8,128)S(1)}, u32[]{:S(2)}, u32[]{:S(2)}) %collective-permute-start.4) | collective-permute-done | bytes 1179680 | tf_op jit(solution)/shard_map/reduce/ppermute | solution.py:227
  70.9 0.1 add.16
  71.2 0.1 clamp_convert_fusion
  71.4 5.7 %collective-permute-start.6 = (s16[9,48,128]{2,1,0:T(8,128)(2,1)S(1)}, s16[9,48,128]{2,1,0:T(8,128)(2,1)S(1)}, u32[]{:S(2)}, u32[]{:S(2)}) collective-permute-start(s16[9,48,128]{2,1,0:T(8,128)(2,1)S(1)} %get-tuple-element.24), channel_id=1, source_target_pairs={{0,64},{64,128},{128,192},{192,256},{256,320},{320,384},{384,448},... | collective-permute-start | bytes 331784 | tf_op jit(solution)/shard_map/reduce/ppermute | solution.py:232
  77.1 2.2 %collective-permute-start.7 = (s16[9,48,128]{2,1,0:T(8,128)(2,1)S(1)}, s16[9,48,128]{2,1,0:T(8,128)(2,1)S(1)}, u32[]{:S(2)}, u32[]{:S(2)}) collective-permute-start(s16[9,48,128]{2,1,0:T(8,128)(2,1)S(1)} %get-tuple-element.25), channel_id=1, source_target_pairs={{0,66},{2,64},{64,130},{66,128},{128,194},{130,192},{192,258},{194... | collective-permute-start | bytes 331784 | tf_op jit(solution)/shard_map/reduce/ppermute | solution.py:238
  79.4 2.8 %collective-permute-start.5 = (s16[17,48,128]{2,1,0:T(8,128)(2,1)S(1)}, s16[17,48,128]{2,1,0:T(8,128)(2,1)S(1)}, u32[]{:S(2)}, u32[]{:S(2)}) collective-permute-start(s16[17,48,128]{2,1,0:T(8,128)(2,1)S(1)} %pad_add_fusion), channel_id=1, source_target_pairs={{0,2},{2,0},{1,3},{3,1},{4,6},{6,4},{5,7},{7,5},{8,10},{10,8},{9,1... | collective-permute-start | bytes 626696 | tf_op jit(solution)/shard_map/reduce/ppermute | solution.py:227
  82.1 0.0 collective-permute-done.6
  82.2 3.8 %collective-permute-done.7 = s16[9,48,128]{2,1,0:T(8,128)(2,1)S(1)} collective-permute-done((s16[9,48,128]{2,1,0:T(8,128)(2,1)S(1)}, s16[9,48,128]{2,1,0:T(8,128)(2,1)S(1)}, u32[]{:S(2)}, u32[]{:S(2)}) %collective-permute-start.7) | collective-permute-done | bytes 110624 | tf_op jit(solution)/shard_map/reduce/ppermute | solution.py:238
  86.0 2.5 %collective-permute-done.5 = s16[17,48,128]{2,1,0:T(8,128)(2,1)S(1)} collective-permute-done((s16[17,48,128]{2,1,0:T(8,128)(2,1)S(1)}, s16[17,48,128]{2,1,0:T(8,128)(2,1)S(1)}, u32[]{:S(2)}, u32[]{:S(2)}) %collective-permute-start.5) | collective-permute-done | bytes 208928 | tf_op jit(solution)/shard_map/reduce/ppermute | solution.py:227
  88.4 0.1 fusion
  88.5 0.1 fusion.5
  88.7 0.1 fusion.4
  88.8 21.6 %all_to_all.11 = s16[16,56,128]{2,1,0:T(8,128)(2,1)S(1)} all-to-all(s16[16,56,128]{2,1,0:T(8,128)(2,1)S(1)} %add_bitcast_fusion), channel_id=1, replica_groups=mesh['region'=8,'z'=16,'yl'=2,'core'=2] {'z'}, dimensions={0} | all-to-all | bytes 458752 | tf_op jit(solution)/shard_map/reduce/all_to_all | solution.py:298
  110.5 0.1 multiply_reduce_fusion
  110.6 0.6 slice_bitcast_fusion.3
  (19 shorter events, 0.4 us)
Async XLA Ops:
  0.6 54.1 %copy-start = (bf16[4,2,256,256]{3,2,1,0:T(8,128)(2,1)S(1)}, bf16[4,2,256,256]{3,2,1,0:T(8,128)(2,1)}, u32[]{:S(2)}) copy-start(bf16[4,2,256,256]{3,2,1,0:T(8,128)(2,1)} %constant.82.clone.tab_ref) | copy-start | bytes 3145732
  0.6 52.7 %copy-start.4 = (s32[1,12,2]{1,2,0:T(2,128)S(1)}, s32[1,12,2]{1,2,0:T(2,128)}, u32[]{:S(2)}) copy-start(s32[1,12,2]{1,2,0:T(2,128)} %param.15) | copy-start | bytes 292
  0.7 54.0 %copy-start.1 = (bf16[1,12,128,128]{3,2,1,0:T(8,128)(2,1)S(1)}, bf16[1,12,128,128]{3,2,1,0:T(8,128)(2,1)}, u32[]{:S(2)}) copy-start(bf16[1,12,128,128]{3,2,1,0:T(8,128)(2,1)} %param.14) | copy-start | bytes 1179652
  0.7 54.0 %copy-start.3 = (f32[128,128]{1,0:T(8,128)S(1)}, f32[128,128]{1,0:T(8,128)}, u32[]{:S(2)}) copy-start(f32[128,128]{1,0:T(8,128)} %probe_imag_ref.1) | copy-start | bytes 196612
  0.7 54.0 %copy-start.2 = (f32[128,128]{1,0:T(8,128)S(1)}, f32[128,128]{1,0:T(8,128)}, u32[]{:S(2)}) copy-start(f32[128,128]{1,0:T(8,128)} %probe_real_ref.1) | copy-start | bytes 196612
  33.0 13.1 %collective-permute-start.2 = (bf16[16,48,128]{2,1,0:T(8,128)(2,1)S(1)}, bf16[16,48,128]{2,1,0:T(8,128)(2,1)S(1)}, u32[]{:S(2)}, u32[]{:S(2)}) collective-permute-start(bf16[16,48,128]{2,1,0:T(8,128)(2,1)S(1)} %all_to_all.10), channel_id=1, source_target_pairs={{0,2},{2,0},{1,3},{3,1},{4,6},{6,4},{5,7},{7,5},{8,10},{10,8},{9,1... | collective-permute-start | bytes 589832 | tf_op jit(solution)/shard_map/gather/ppermute | solution.py:227
  36.5 7.7 %collective-permute-start = (bf16[8,48,128]{2,1,0:T(8,128)(2,1)S(1)}, bf16[8,48,128]{2,1,0:T(8,128)(2,1)S(1)}, u32[]{:S(2)}, u32[]{:S(2)}) collective-permute-start(bf16[8,48,128]{2,1,0:T(8,128)(2,1)S(1)} %slice.95), channel_id=1, source_target_pairs={{0,450},{2,448},{64,2},{66,0},{128,66},{130,64},{192,130},{194,128... | collective-permute-start | bytes 294920 | tf_op jit(solution)/shard_map/gather/ppermute | solution.py:238
  44.2 6.5 %collective-permute-start.1 = (bf16[8,48,128]{2,1,0:T(8,128)(2,1)S(1)}, bf16[8,48,128]{2,1,0:T(8,128)(2,1)S(1)}, u32[]{:S(2)}, u32[]{:S(2)}) collective-permute-start(bf16[8,48,128]{2,1,0:T(8,128)(2,1)S(1)} %collective-permute-done), channel_id=1, source_target_pairs={{0,2},{2,0},{1,3},{3,1},{4,6},{6,4},{5,7},{7,5},{8,10},{10,8},{9,1... | collective-permute-start | bytes 294920 | tf_op jit(solution)/shard_map/gather/ppermute | solution.py:227
  50.8 3.9 %collective-permute-start.3 = (bf16[2,24,48,128]{3,2,1,0:T(8,128)(2,1)S(1)}, bf16[2,24,48,128]{3,2,1,0:T(8,128)(2,1)S(1)}, u32[]{:S(2)}, u32[]{:S(2)}) collective-permute-start(bf16[2,24,48,128]{3,2,1,0:T(8,128)(2,1)S(1)} %bitcast.49), channel_id=1, source_target_pairs={{0,1},{1,0},{2,3},{3,2},{4,5},{5,4},{6,7},{7,6},{8,9},{9,8},{10,11... | collective-permute-start | bytes 1769480 | tf_op jit(solution)/shard_map/gather/ppermute | solution.py:227
  66.2 4.7 %collective-permute-start.4 = (f32[2,24,48,128]{3,2,1,0:T(8,128)S(1)}, f32[2,24,48,128]{3,2,1,0:T(8,128)S(1)}, u32[]{:S(2)}, u32[]{:S(2)}) collective-permute-start(f32[2,24,48,128]{3,2,1,0:T(8,128)S(1)} %get-tuple-element.17), channel_id=1, source_target_pairs={{0,1},{1,0},{2,3},{3,2},{4,5},{5,4},{6,7},{7,6},{8,9},{9,8},{10,11... | collective-permute-start | bytes 3538952 | tf_op jit(solution)/shard_map/reduce/ppermute | solution.py:227
  71.4 10.7 %collective-permute-start.6 = (s16[9,48,128]{2,1,0:T(8,128)(2,1)S(1)}, s16[9,48,128]{2,1,0:T(8,128)(2,1)S(1)}, u32[]{:S(2)}, u32[]{:S(2)}) collective-permute-start(s16[9,48,128]{2,1,0:T(8,128)(2,1)S(1)} %get-tuple-element.24), channel_id=1, source_target_pairs={{0,64},{64,128},{128,192},{192,256},{256,320},{320,384},{384,448},... | collective-permute-start | bytes 331784 | tf_op jit(solution)/shard_map/reduce/ppermute | solution.py:232
  77.1 8.8 %collective-permute-start.7 = (s16[9,48,128]{2,1,0:T(8,128)(2,1)S(1)}, s16[9,48,128]{2,1,0:T(8,128)(2,1)S(1)}, u32[]{:S(2)}, u32[]{:S(2)}) collective-permute-start(s16[9,48,128]{2,1,0:T(8,128)(2,1)S(1)} %get-tuple-element.25), channel_id=1, source_target_pairs={{0,66},{2,64},{64,130},{66,128},{128,194},{130,192},{192,258},{194... | collective-permute-start | bytes 331784 | tf_op jit(solution)/shard_map/reduce/ppermute | solution.py:238
  79.4 9.0 %collective-permute-start.5 = (s16[17,48,128]{2,1,0:T(8,128)(2,1)S(1)}, s16[17,48,128]{2,1,0:T(8,128)(2,1)S(1)}, u32[]{:S(2)}, u32[]{:S(2)}) collective-permute-start(s16[17,48,128]{2,1,0:T(8,128)(2,1)S(1)} %pad_add_fusion), channel_id=1, source_target_pairs={{0,2},{2,0},{1,3},{3,1},{4,6},{6,4},{5,7},{7,5},{8,10},{10,8},{9,1... | collective-permute-start | bytes 626696 | tf_op jit(solution)/shard_map/reduce/ppermute | solution.py:227

commit v4 on v3

--- a/solution.py
+++ b/solution.py
@@ -103,8 +103,8 @@
     probe_imag_ref,
     pat_ref,
     tab_ref,
-    near_ref,
-    far_ref,
+    own_ref,
+    next_ref,
     keep_ref,
     send_ref,
     obj_ref,
@@ -122,19 +122,24 @@
     def eight_rows(y, z):
         return pl.ds(pl.multiple_of((2 * z + lax.rem(y + yl, 2)) * 2 * half, 2 * half), 2 * half)
 
-    def unpack(z, _):
+    def place(low, high, rows):
+        low, high = low.astype(jnp.float32), high.astype(jnp.float32)
+        for s in range(slices):
+            for h in range(2):
+                k = (s * 2 + h) * 2 * half
+                a, b = low[k : k + 2 * half], high[k : k + 2 * half]
+                obj_ref[0, s, h, rows, :] = jnp.where(top, a, pltpu.roll(b, half, 0))
+                obj_ref[1, s, h, rows, :] = jnp.where(top, pltpu.roll(a, half, 0), b)
+
+    def unpack_own(z, _):
         for y in range(2):
-            rows = eight_rows(y, z)
-            near = near_ref[y, z].astype(jnp.float32)
-            far = far_ref[y, z].astype(jnp.float32)
-            low = jnp.where(first_core, near, far)
-            high = jnp.where(first_core, far, near)
-            for s in range(slices):
-                for h in range(2):
-                    k = (s * 2 + h) * 2 * half
-                    a, b = low[k : k + 2 * half], high[k : k + 2 * half]
-                    obj_ref[0, s, h, rows, :] = jnp.where(top, a, pltpu.roll(b, half, 0))
-                    obj_ref[1, s, h, rows, :] = jnp.where(top, pltpu.roll(a, half, 0), b)
+            row = pl.multiple_of((2 * z + y) * 2 * half, 2 * half)
+            place(own_ref[2 * y, z], own_ref[2 * y + 1, z], pl.ds(row, 2 * half))
+        return 0
+
+    def unpack_next(z, _):
+        for y in range(2):
+            place(next_ref[0, y, z], next_ref[1, y, z], eight_rows(y, z + own_ref.shape[1]))
         return 0
 
     def pack(z, _):
@@ -151,8 +156,8 @@
                     send_ref[y, z, k : k + 2 * half] = jnp.where(first_core, high, low)
         return 0
 
-    blocks = near_ref.shape[1]
-    lax.fori_loop(0, blocks, unpack, 0)
+    lax.fori_loop(0, own_ref.shape[1], unpack_own, 0)
+    lax.fori_loop(0, next_ref.shape[2], unpack_next, 0)
 
     count = cnt_ref[0, 0]
     lane = lax.broadcasted_iota(jnp.int32, (w, w), 1)
@@ -186,7 +191,8 @@
                 wave = transform(tab_ref, PROP, False, leaving)
         far = transform(tab_ref, DFT, False, leaving)
         misfit = [
-            r * r + i * i - pat_ref[n].astype(jnp.float32) for r, i, n in zip(*far, numbers)
+            (r * r + i * i - pat_ref[n].astype(jnp.float32)) * weight
+            for r, i, n, weight in zip(*far, numbers, weights)
         ]
         back = ([m * r for m, r in zip(misfit, far[0])], [m * i for m, i in zip(misfit, far[1])])
         back = transform(tab_ref, DFT, True, back)
@@ -194,7 +200,7 @@
             term = conj_mul(waves[s], back)
             for part in range(2):
                 for k in range(GROUP):
-                    moved = pltpu.roll(term[part][k] * weights[k], turn[k], 1)
+                    moved = pltpu.roll(term[part][k], turn[k], 1)
                     here = lane >= cols[k]
                     grad_ref[part, s, 0, pl.ds(rows[k], w), :] += jnp.where(here, moved, 0.0)
                     grad_ref[part, s, 1, pl.ds(rows[k], w), :] += jnp.where(here, 0.0, moved)
@@ -203,24 +209,26 @@
         return 0
 
     lax.fori_loop(0, lax.div(count + (GROUP - 1), GROUP), visit, 0)
-    lax.fori_loop(0, blocks, pack, 0)
-
-
-def slots_call(scale, place, offsets, counts, probe, patterns, tables, near, far):
+    lax.fori_loop(0, keep_ref.shape[1], pack, 0)
+
+
+def slots_call(scale, place, offsets, counts, probe, patterns, tables, own, following):
     slices = 3
     width = probe[0].shape[0]
     vector = pl.BlockSpec(memory_space=pltpu.VMEM)
     scalar = pl.BlockSpec(memory_space=pltpu.SMEM)
-    held = pltpu.VMEM((2, slices, 2, near.shape[1] * 16, width), jnp.float32)
+    blocks = own.shape[1] + following.shape[2]
+    held = pltpu.VMEM((2, slices, 2, blocks * 16, width), jnp.float32)
+    out = jax.ShapeDtypeStruct((2, blocks) + own.shape[2:], jnp.float32)
     return pl.pallas_call(
         functools.partial(slots_kernel, scale),
-        out_shape=[jax.ShapeDtypeStruct(near.shape, jnp.float32)] * 2,
+        out_shape=[out] * 2,
         in_specs=[scalar] * 3 + [vector] * 6,
         out_specs=[vector] * 2,
         scratch_shapes=[held, held],
         compiler_params=pltpu.CompilerParams(vmem_limit_bytes=44 * 1024 * 1024),
         name="slots",
-    )(place, offsets, counts, *probe, patterns, tables, near, far)
+    )(place, offsets, counts, *probe, patterns, tables, own, following)
 
 
 def swap(block, axis):
@@ -238,17 +246,21 @@
     return lax.ppermute(block, ("region", "yl"), route)
 
 
-def encode(blocks, over):
-    most = jnp.max(jnp.abs(blocks), axis=over, keepdims=True)
+def encode(blocks):
+    most = jnp.max(jnp.abs(blocks), axis=(0, 1), keepdims=True)
     code = jnp.ceil(jnp.log2(jnp.maximum(most, 1e-37)) * 64.0)
     share = jnp.clip(jnp.round(blocks * jnp.exp2(code / -64.0) * 32767.0), -32767.0, 32767.0)
     return share.astype(jnp.int16), code[0].astype(jnp.int16)
 
 
-def decode(message, axis):
-    code = lax.slice_in_dim(message, message.shape[axis] - 1, None, axis=axis)
-    share = lax.slice_in_dim(message, 0, message.shape[axis] - 1, axis=axis)
+def decode(share, code):
     return share.astype(jnp.float32) * (jnp.exp2(code.astype(jnp.float32) / 64.0) / 32767.0)
+
+
+def carry(send, share, code):
+    tile = code.shape[-2:]
+    moved = send(jnp.concatenate([share.reshape(-1, *tile), code]))
+    return decode(moved[:-1], moved[-1]).reshape(share.shape)
 
 
 def local(tables, object_real, object_imag, probe_real, probe_imag, patterns, offsets, counts):
@@ -267,36 +279,30 @@
         column = lax.all_to_all(
             jnp.broadcast_to(block, (depth, packed, width)), "z", 0, 0, tiled=True
         )
-        other = swap(column, "yl")
-        following_other = shift_and_swap(column[:below], -1)
-        following = swap(following_other, "yl")
-        near = jnp.concatenate([column, following, other, following_other])
-        near = near.reshape(2, depth + below, packed, width)
-        far = swap(near, "core")
+        column, offsets, place = lax.optimization_barrier((column, offsets, place))
+        following = jnp.stack([shift(column[:below], -1), shift_and_swap(column[:below], -1)])
+        own = lax.all_gather(column, ("yl", "core"), axis=0)
+        following = lax.all_gather(following, "core", axis=0)
 
     keep, send = slots_call(
-        scale, place, offsets, counts, (probe_real, probe_imag), patterns[0], tables, near, far
+        scale, place, offsets, counts, (probe_real, probe_imag), patterns[0], tables, own, following
     )
 
     with jax.named_scope("reduce"):
         total = keep + swap(send, "core")
+        total = total.reshape(2, depth + below, -1, 2 * rows, width)
         away = jnp.concatenate([total[1], total[0, depth:]])
-        share, code = encode(away, (0,))
-        code = code[None]
-        near_next = jnp.concatenate([share[depth + below :], code])
-        far_next = jnp.concatenate([share[depth : depth + below], code])
-        beside = jnp.concatenate([share[:depth], code])
-        far_next = shift_and_swap(far_next, 1)
-        near_next = shift(near_next, 1)
-        beside = swap(beside, "yl")
-        total = total[0, :depth] + decode(beside, 0)
-        total = total.at[:below].add(decode(near_next, 0) + decode(far_next, 0))
-        total = total.reshape(depth, -1, 2 * rows, width)
-        share, code = encode(total, (0, 1))
+        share, code = encode(away)
+        near_next = carry(lambda x: shift(x, 1), share[depth + below :], code)
+        far_next = carry(lambda x: shift_and_swap(x, 1), share[depth : depth + below], code)
+        beside = carry(lambda x: swap(x, "yl"), share[:depth], code)
+        total = (total[0, :depth] + beside).at[:below].add(near_next + far_next)
+        share, code = encode(total)
         code = jnp.broadcast_to(code, (depth,) + code.shape)
-        message = jnp.concatenate([share, code], axis=1).reshape(depth, -1, width)
-        message = lax.all_to_all(message, "z", 0, 0, tiled=True)
-        total = decode(message.reshape(depth, -1, 2 * rows, width), 1).sum(0)
+        parts = jnp.concatenate([share, code], axis=1).reshape(depth, -1, width)
+        parts = lax.all_to_all(parts, "z", 0, 0, tiled=True)
+        parts = parts.reshape(depth, -1, 2 * rows, width)
+        total = decode(parts[:, :-1], parts[:, -1:]).sum(0)
         total = total.reshape(slices, halves, 2, rows, width).transpose(2, 0, 3, 1, 4)
         total = total.reshape(2, slices, rows, columns)
     return total[0], total[1]

time: 112 us -> 110 us (0.982)
  blocking collectives: 53 us -> 32.3 us
  starting transfers between devices: 24.3 us -> 35.5 us
  waiting for transfers between devices: 18.1 us -> 24.9 us
    all_to_all x2 -> x1, blocking collectives: 53 us -> 21.6 us  [local(): parts = lax.all_to_all(parts, 'z', 0, 0, tiled=True)]
    all_to_all x0 -> x1, waiting for transfers between devices: none -> 15.5 us  [local(): lax.all_to_all(jnp.broadcast_to(block, (depth, packed, width)), 'z', 0, 0...]
    all_to_all x0 -> x1, starting transfers between devices: none -> 15.2 us  [local(): lax.all_to_all(jnp.broadcast_to(block, (depth, packed, width)), 'z', 0, 0...]
    all_gather x0 -> x2, blocking collectives: none -> 10.7 us  [the longest x1 8.61 us: local(): own = lax.all_gather(column, ('yl', 'core'), axis=0)]
    ppermute x5 -> x2, starting transfers between devices: 12 us -> 3.84 us  [swap(): return lax.ppermute(block, axis, [(0, 1), (1, 0)])]
    ppermute x2, waiting for transfers between devices: 7.11 us -> 2.6 us  [shift_and_swap(): return lax.ppermute(block, ('region', 'yl'), route)]
    ppermute x5 -> x2, waiting for transfers between devices: 11 us -> 6.71 us  [swap(): return lax.ppermute(block, axis, [(0, 1), (1, 0)])]
    ppermute x2, starting transfers between devices: 6.59 us -> 9.41 us  [shift_and_swap(): return lax.ppermute(block, ('region', 'yl'), route)]
  transfers between devices with their start and end apart: 8 -> 7, of which waited for: 6 -> 4; matrix products, arithmetic and copies ran while one was open for 0% -> 0% of each run, Pallas kernels for 0% -> 0%
where the time goes in v4:
time: 110 us; the launch traced here: 109 us
  starting transfers between devices  35.5 us (32%)
  blocking collectives  32.3 us (29%)
  waiting for transfers between devices  24.9 us (23%)
  Pallas kernels  11.3 us (10%)
  other arithmetic  1.72 us (2%)
  between operations  1.67 us (2%)
  local copies, waits for them, and re-layouts  1.53 us (1%)
    all_to_all x1, blocking collectives, local(): parts = lax.all_to_all(parts, 'z', 0, 0, tiled=True)  21.6 us
    all_to_all x1, waiting for transfers between devices, local(): lax.all_to_all(jnp.broadcast_to(block, (depth, packed, width)), 'z', 0, 0...  15.5 us
    all_to_all x1, starting transfers between devices, local(): lax.all_to_all(jnp.broadcast_to(block, (depth, packed, width)), 'z', 0, 0...  15.2 us
    pallas_call x1, Pallas kernels, slots_call(): pl.pallas_call(functools.partial(slots_kernel, scale), out_shape=[out] *...  11.3 us
    ppermute x2, starting transfers between devices, shift_and_swap(): return lax.ppermute(block, ('region', 'yl'), route)  9.41 us
    all_gather x1, blocking collectives, local(): own = lax.all_gather(column, ('yl', 'core'), axis=0)  8.61 us
    ppermute x2, starting transfers between devices, shift(): lax.ppermute(block, 'region', [(i, (i + distance) % bands) for i in range...  7.02 us
    ppermute x2, waiting for transfers between devices, swap(): return lax.ppermute(block, axis, [(0, 1), (1, 0)])  6.71 us
  transfers between devices with their start and end apart: 7, of which 4 were waited for; matrix products, arithmetic and copies ran while one was open for 0% of the time, Pallas kernels for 0%

profile of v4, /device:TPU:6, one launch (start us, length us, event | category | flops | bytes accessed | tf_op | source)
XLA Modules:
  0.0 108.8 jit_solution(17033224787846854699)
XLA Ops:
  0.6 0.0 copy-start.4
  0.6 0.7 pad_maximum_fusion.2
  1.4 0.7 broadcast_in_dim.4
  2.1 15.2 %all-to-all-start = ((bf16[16,48,128]{2,1,0:T(8,128)(2,1)}), bf16[16,48,128]{2,1,0:T(8,128)(2,1)S(1)}, u32[]{:S(2)}, u32[]{:S(2)}) async-start(bf16[16,48,128]{2,1,0:T(8,128)(2,1)} %broadcast_in_dim.4), calls=%async_computation | async-start | bytes 393216 | tf_op jit(solution)/shard_map/gather/all_to_all | solution.py:279
  17.3 0.0 copy-start
  17.3 0.0 copy-start.1
  17.3 0.0 copy-start.2
  17.3 0.0 copy-start.3
  18.1 0.1 pad_add_fusion.3.place_ref
  18.2 15.5 %all-to-all-done = bf16[16,48,128]{2,1,0:T(8,128)(2,1)S(1)} async-done(((bf16[16,48,128]{2,1,0:T(8,128)(2,1)}), bf16[16,48,128]{2,1,0:T(8,128)(2,1)S(1)}, u32[]{:S(2)}, u32[]{:S(2)}) %all-to-all-start) | async-done | bytes 196640 | tf_op jit(solution)/shard_map/gather/all_to_all | solution.py:279
  33.7 5.2 %collective-permute-start.1 = (bf16[8,48,128]{2,1,0:T(8,128)(2,1)S(1)}, bf16[8,48,128]{2,1,0:T(8,128)(2,1)S(1)}, u32[]{:S(2)}, u32[]{:S(2)}) collective-permute-start(bf16[8,48,128]{2,1,0:T(8,128)(2,1)S(1)} %slice.84), channel_id=1, source_target_pairs={{0,450},{2,448},{64,2},{66,0},{128,66},{130,64},{192,130},{194,128... | collective-permute-start | bytes 294920 | tf_op jit(solution)/shard_map/gather/ppermute | solution.py:246
  38.9 2.5 %collective-permute-start = (bf16[8,48,128]{2,1,0:T(8,128)(2,1)S(1)}, bf16[8,48,128]{2,1,0:T(8,128)(2,1)S(1)}, u32[]{:S(2)}, u32[]{:S(2)}) collective-permute-start(bf16[8,48,128]{2,1,0:T(8,128)(2,1)S(1)} %slice.84), channel_id=1, source_target_pairs={{0,448},{64,0},{128,64},{192,128},{256,192},{320,256},{384,320},{4... | collective-permute-start | bytes 294920 | tf_op jit(solution)/shard_map/gather/ppermute | solution.py:240
  41.5 8.6 %all-gather = bf16[64,48,128]{2,1,0:T(8,128)(2,1)S(1)} all-gather(bf16[16,48,128]{2,1,0:T(8,128)(2,1)S(1)} %all-to-all-done), channel_id=2, replica_groups=mesh['region'=8,'z'=16,'yl'=2,'core'=2] {'yl','core'}, dimensions={0}, use_global_device_ids=true | all-gather | bytes 983040 | tf_op jit(solution)/shard_map/gather/all_gather | solution.py:284
  50.1 0.0 copy-done.4
  50.1 0.1 copy.16.off_ref
  50.2 0.0 collective-permute-done.1
  50.2 0.0 collective-permute-done
  50.2 2.1 %all-gather.1 = bf16[4,8,48,128]{3,2,1,0:T(8,128)(2,1)S(1)} all-gather(bf16[2,8,48,128]{3,2,1,0:T(8,128)(2,1)S(1)} %pad_maximum_fusion.1), channel_id=3, replica_groups=mesh['region'=8,'z'=16,'yl'=2,'core'=2] {'core'}, dimensions={0}, use_global_device_ids=true | all-gather | bytes 589824 | tf_op jit(solution)/shard_map/gather/all_gather | solution.py:285
  52.3 0.0 copy-done
  52.3 0.0 copy-done.1
  52.3 0.0 copy-done.2
  52.3 0.0 copy-done.3
  52.3 11.3 %slots.1 = (f32[2,24,48,128]{3,2,1,0:T(8,128)S(1)}, f32[2,24,48,128]{3,2,1,0:T(8,128)S(1)}) custom-call(s32[2]{0:T(128)S(1)} %pad_add_fusion.3.place_ref, s32[1,12,2]{2,1,0:T(8,128)S(1)} %copy.16.off_ref, s32[1,1]{1,0:T(1,128)S(6)} %copy.18.cnt_ref, f32[128,128]{1,0:T(8,128)S(1)} %copy-done.2, f32[128,128]{1,0:T(8,128)S(1)} %copy-done.3, ...), custom_call_target="tpu_custom_call" | custom-call | tf_op jit(solution)/shard_map/slots/pallas_call | solution.py:223
  63.6 1.9 %collective-permute-start.2 = (f32[2,24,48,128]{3,2,1,0:T(8,128)S(1)}, f32[2,24,48,128]{3,2,1,0:T(8,128)S(1)}, u32[]{:S(2)}, u32[]{:S(2)}) collective-permute-start(f32[2,24,48,128]{3,2,1,0:T(8,128)S(1)} %get-tuple-element.23), channel_id=1, source_target_pairs={{0,1},{1,0},{2,3},{3,2},{4,5},{5,4},{6,7},{7,6},{8,9},{9,8},{10,11... | collective-permute-start | bytes 3538952 | tf_op jit(solution)/shard_map/reduce/ppermute | solution.py:235
  65.5 2.8 %collective-permute-done.2 = f32[2,24,48,128]{3,2,1,0:T(8,128)S(1)} collective-permute-done((f32[2,24,48,128]{3,2,1,0:T(8,128)S(1)}, f32[2,24,48,128]{3,2,1,0:T(8,128)S(1)}, u32[]{:S(2)}, u32[]{:S(2)}) %collective-permute-start.2) | collective-permute-done | bytes 1179680 | tf_op jit(solution)/shard_map/reduce/ppermute | solution.py:235
  68.4 0.1 add.19
  68.6 0.1 abs_reduce_fusion
  68.6 0.1 clamp_convert_fusion
  68.9 4.5 %collective-permute-start.4 = (s16[49,8,128]{2,1,0:T(8,128)(2,1)S(1)}, s16[49,8,128]{2,1,0:T(8,128)(2,1)S(1)}, u32[]{:S(2)}, u32[]{:S(2)}) collective-permute-start(s16[49,8,128]{2,1,0:T(8,128)(2,1)S(1)} %get-tuple-element.32), channel_id=1, source_target_pairs={{0,64},{64,128},{128,192},{192,256},{256,320},{320,384},{384,448},... | collective-permute-start | bytes 301064 | tf_op jit(solution)/shard_map/reduce/ppermute | solution.py:240
  73.4 4.2 %collective-permute-start.5 = (s16[49,8,128]{2,1,0:T(8,128)(2,1)S(1)}, s16[49,8,128]{2,1,0:T(8,128)(2,1)S(1)}, u32[]{:S(2)}, u32[]{:S(2)}) collective-permute-start(s16[49,8,128]{2,1,0:T(8,128)(2,1)S(1)} %get-tuple-element.33), channel_id=1, source_target_pairs={{0,66},{2,64},{64,130},{66,128},{128,194},{130,192},{192,258},{194... | collective-permute-start | bytes 301064 | tf_op jit(solution)/shard_map/reduce/ppermute | solution.py:246
  77.6 1.9 %collective-permute-start.3 = (s16[97,8,128]{2,1,0:T(8,128)(2,1)S(1)}, s16[97,8,128]{2,1,0:T(8,128)(2,1)S(1)}, u32[]{:S(2)}, u32[]{:S(2)}) collective-permute-start(s16[97,8,128]{2,1,0:T(8,128)(2,1)S(1)} %pad_add_fusion), channel_id=1, source_target_pairs={{0,2},{2,0},{1,3},{3,1},{4,6},{6,4},{5,7},{7,5},{8,10},{10,8},{9,1... | collective-permute-start | bytes 595976 | tf_op jit(solution)/shard_map/reduce/ppermute | solution.py:235
  79.5 0.0 collective-permute-done.4
  79.6 2.6 %collective-permute-done.5 = s16[49,8,128]{2,1,0:T(8,128)(2,1)S(1)} collective-permute-done((s16[49,8,128]{2,1,0:T(8,128)(2,1)S(1)}, s16[49,8,128]{2,1,0:T(8,128)(2,1)S(1)}, u32[]{:S(2)}, u32[]{:S(2)}) %collective-permute-start.5) | collective-permute-done | bytes 100384 | tf_op jit(solution)/shard_map/reduce/ppermute | solution.py:246
  82.2 0.1 multiply_add_fusion
  82.3 3.9 %collective-permute-done.3 = s16[97,8,128]{2,1,0:T(8,128)(2,1)S(1)} collective-permute-done((s16[97,8,128]{2,1,0:T(8,128)(2,1)S(1)}, s16[97,8,128]{2,1,0:T(8,128)(2,1)S(1)}, u32[]{:S(2)}, u32[]{:S(2)}) %collective-permute-start.3) | collective-permute-done | bytes 198688 | tf_op jit(solution)/shard_map/reduce/ppermute | solution.py:235
  86.2 0.1 convert_multiply_fusion
  86.2 0.1 fusion
  86.4 0.1 clamp_convert_fusion.1
  86.5 21.6 %all_to_all.10 = s16[16,56,128]{2,1,0:T(8,128)(2,1)S(1)} all-to-all(s16[16,56,128]{2,1,0:T(8,128)(2,1)S(1)} %add_bitcast_fusion), channel_id=1, replica_groups=mesh['region'=8,'z'=16,'yl'=2,'core'=2] {'z'}, dimensions={0} | all-to-all | bytes 458752 | tf_op jit(solution)/shard_map/reduce/all_to_all | solution.py:303
  108.1 0.1 multiply_reduce_fusion
  108.2 0.6 slice_bitcast_fusion.3
  (18 shorter events, 0.3 us)
Async XLA Ops:
  0.6 49.4 %copy-start.4 = (s32[1,12,2]{1,2,0:T(2,128)S(1)}, s32[1,12,2]{1,2,0:T(2,128)}, u32[]{:S(2)}) copy-start(s32[1,12,2]{1,2,0:T(2,128)} %param.15) | copy-start | bytes 292
  2.1 31.6 %all-to-all-start = ((bf16[16,48,128]{2,1,0:T(8,128)(2,1)}), bf16[16,48,128]{2,1,0:T(8,128)(2,1)S(1)}, u32[]{:S(2)}, u32[]{:S(2)}) async-start(bf16[16,48,128]{2,1,0:T(8,128)(2,1)} %broadcast_in_dim.4), calls=%async_computation | async-start | bytes 393216 | tf_op jit(solution)/shard_map/gather/all_to_all | solution.py:279
  17.3 35.0 %copy-start = (bf16[4,2,256,256]{3,2,1,0:T(8,128)(2,1)S(1)}, bf16[4,2,256,256]{3,2,1,0:T(8,128)(2,1)}, u32[]{:S(2)}) copy-start(bf16[4,2,256,256]{3,2,1,0:T(8,128)(2,1)} %constant.79.clone.tab_ref) | copy-start | bytes 3145732
  17.3 35.0 %copy-start.1 = (bf16[1,12,128,128]{3,2,1,0:T(8,128)(2,1)S(1)}, bf16[1,12,128,128]{3,2,1,0:T(8,128)(2,1)}, u32[]{:S(2)}) copy-start(bf16[1,12,128,128]{3,2,1,0:T(8,128)(2,1)} %param.14) | copy-start | bytes 1179652
  17.3 35.0 %copy-start.2 = (f32[128,128]{1,0:T(8,128)S(1)}, f32[128,128]{1,0:T(8,128)}, u32[]{:S(2)}) copy-start(f32[128,128]{1,0:T(8,128)} %probe_real_ref.1) | copy-start | bytes 196612
  17.3 35.0 %copy-start.3 = (f32[128,128]{1,0:T(8,128)S(1)}, f32[128,128]{1,0:T(8,128)}, u32[]{:S(2)}) copy-start(f32[128,128]{1,0:T(8,128)} %probe_imag_ref.1) | copy-start | bytes 196612
  33.7 16.5 %collective-permute-start.1 = (bf16[8,48,128]{2,1,0:T(8,128)(2,1)S(1)}, bf16[8,48,128]{2,1,0:T(8,128)(2,1)S(1)}, u32[]{:S(2)}, u32[]{:S(2)}) collective-permute-start(bf16[8,48,128]{2,1,0:T(8,128)(2,1)S(1)} %slice.84), channel_id=1, source_target_pairs={{0,450},{2,448},{64,2},{66,0},{128,66},{130,64},{192,130},{194,128... | collective-permute-start | bytes 294920 | tf_op jit(solution)/shard_map/gather/ppermute | solution.py:246
  38.9 11.3 %collective-permute-start = (bf16[8,48,128]{2,1,0:T(8,128)(2,1)S(1)}, bf16[8,48,128]{2,1,0:T(8,128)(2,1)S(1)}, u32[]{:S(2)}, u32[]{:S(2)}) collective-permute-start(bf16[8,48,128]{2,1,0:T(8,128)(2,1)S(1)} %slice.84), channel_id=1, source_target_pairs={{0,448},{64,0},{128,64},{192,128},{256,192},{320,256},{384,320},{4... | collective-permute-start | bytes 294920 | tf_op jit(solution)/shard_map/gather/ppermute | solution.py:240
  63.6 4.7 %collective-permute-start.2 = (f32[2,24,48,128]{3,2,1,0:T(8,128)S(1)}, f32[2,24,48,128]{3,2,1,0:T(8,128)S(1)}, u32[]{:S(2)}, u32[]{:S(2)}) collective-permute-start(f32[2,24,48,128]{3,2,1,0:T(8,128)S(1)} %get-tuple-element.23), channel_id=1, source_target_pairs={{0,1},{1,0},{2,3},{3,2},{4,5},{5,4},{6,7},{7,6},{8,9},{9,8},{10,11... | collective-permute-start | bytes 3538952 | tf_op jit(solution)/shard_map/reduce/ppermute | solution.py:235
  68.9 10.7 %collective-permute-start.4 = (s16[49,8,128]{2,1,0:T(8,128)(2,1)S(1)}, s16[49,8,128]{2,1,0:T(8,128)(2,1)S(1)}, u32[]{:S(2)}, u32[]{:S(2)}) collective-permute-start(s16[49,8,128]{2,1,0:T(8,128)(2,1)S(1)} %get-tuple-element.32), channel_id=1, source_target_pairs={{0,64},{64,128},{128,192},{192,256},{256,320},{320,384},{384,448},... | collective-permute-start | bytes 301064 | tf_op jit(solution)/shard_map/reduce/ppermute | solution.py:240
  73.4 8.8 %collective-permute-start.5 = (s16[49,8,128]{2,1,0:T(8,128)(2,1)S(1)}, s16[49,8,128]{2,1,0:T(8,128)(2,1)S(1)}, u32[]{:S(2)}, u32[]{:S(2)}) collective-permute-start(s16[49,8,128]{2,1,0:T(8,128)(2,1)S(1)} %get-tuple-element.33), channel_id=1, source_target_pairs={{0,66},{2,64},{64,130},{66,128},{128,194},{130,192},{192,258},{194... | collective-permute-start | bytes 301064 | tf_op jit(solution)/shard_map/reduce/ppermute | solution.py:246
  77.6 8.5 %collective-permute-start.3 = (s16[97,8,128]{2,1,0:T(8,128)(2,1)S(1)}, s16[97,8,128]{2,1,0:T(8,128)(2,1)S(1)}, u32[]{:S(2)}, u32[]{:S(2)}) collective-permute-start(s16[97,8,128]{2,1,0:T(8,128)(2,1)S(1)} %pad_add_fusion), channel_id=1, source_target_pairs={{0,2},{2,0},{1,3},{3,1},{4,6},{6,4},{5,7},{7,5},{8,10},{10,8},{9,1... | collective-permute-start | bytes 595976 | tf_op jit(solution)/shard_map/reduce/ppermute | solution.py:235

commit v5 on v4

--- a/solution.py
+++ b/solution.py
@@ -156,8 +156,8 @@
                     send_ref[y, z, k : k + 2 * half] = jnp.where(first_core, high, low)
         return 0
 
-    lax.fori_loop(0, own_ref.shape[1], unpack_own, 0)
-    lax.fori_loop(0, next_ref.shape[2], unpack_next, 0)
+    lax.fori_loop(0, own_ref.shape[1], unpack_own, 0, unroll=4)
+    lax.fori_loop(0, next_ref.shape[2], unpack_next, 0, unroll=4)
 
     count = cnt_ref[0, 0]
     lane = lax.broadcasted_iota(jnp.int32, (w, w), 1)
@@ -209,7 +209,7 @@
         return 0
 
     lax.fori_loop(0, lax.div(count + (GROUP - 1), GROUP), visit, 0)
-    lax.fori_loop(0, keep_ref.shape[1], pack, 0)
+    lax.fori_loop(0, keep_ref.shape[1], pack, 0, unroll=4)
 
 
 def slots_call(scale, place, offsets, counts, probe, patterns, tables, own, following):

time: 110 us -> 110 us (level)
  no operation moved by 1% of the time
where the time goes in v5:
time: 110 us; the launch traced here: 108 us
  starting transfers between devices  35.9 us (33%)
  blocking collectives  32.3 us (29%)
  waiting for transfers between devices  24.3 us (22%)
  Pallas kernels  11 us (10%)
  other arithmetic  1.72 us (2%)
  between operations  1.67 us (2%)
  local copies, waits for them, and re-layouts  1.53 us (1%)
    all_to_all x1, blocking collectives, local(): parts = lax.all_to_all(parts, 'z', 0, 0, tiled=True)  21.6 us
    all_to_all x1, waiting for transfers between devices, local(): lax.all_to_all(jnp.broadcast_to(block, (depth, packed, width)), 'z', 0, 0...  15.5 us
    all_to_all x1, starting transfers between devices, local(): lax.all_to_all(jnp.broadcast_to(block, (depth, packed, width)), 'z', 0, 0...  15.2 us
    pallas_call x1, Pallas kernels, slots_call(): pl.pallas_call(functools.partial(slots_kernel, scale), out_shape=[out] *...  11 us
    ppermute x2, starting transfers between devices, shift_and_swap(): return lax.ppermute(block, ('region', 'yl'), route)  9.44 us
    all_gather x1, blocking collectives, local(): own = lax.all_gather(column, ('yl', 'core'), axis=0)  8.61 us
    ppermute x2, starting transfers between devices, shift(): lax.ppermute(block, 'region', [(i, (i + distance) % bands) for i in range...  7.1 us
    ppermute x2, waiting for transfers between devices, swap(): return lax.ppermute(block, axis, [(0, 1), (1, 0)])  6.2 us
  transfers between devices with their start and end apart: 7, of which 4 were waited for; matrix products, arithmetic and copies ran while one was open for 0% of the time, Pallas kernels for 0%

profile of v5, /device:TPU:6, one launch (start us, length us, event | category | flops | bytes accessed | tf_op | source)
XLA Modules:
  0.0 108.4 jit_solution(4026406127958399522)
XLA Ops:
  0.6 0.0 copy-start.4
  0.6 0.7 pad_maximum_fusion.2
  1.4 0.7 broadcast_in_dim.4
  2.1 15.2 %all-to-all-start = ((bf16[16,48,128]{2,1,0:T(8,128)(2,1)}), bf16[16,48,128]{2,1,0:T(8,128)(2,1)S(1)}, u32[]{:S(2)}, u32[]{:S(2)}) async-start(bf16[16,48,128]{2,1,0:T(8,128)(2,1)} %broadcast_in_dim.4), calls=%async_computation | async-start | bytes 393216 | tf_op jit(solution)/shard_map/gather/all_to_all | solution.py:279
  17.3 0.0 copy-start
  17.3 0.0 copy-start.1
  17.3 0.0 copy-start.2
  17.3 0.0 copy-start.3
  18.1 0.1 pad_add_fusion.3.place_ref
  18.2 15.5 %all-to-all-done = bf16[16,48,128]{2,1,0:T(8,128)(2,1)S(1)} async-done(((bf16[16,48,128]{2,1,0:T(8,128)(2,1)}), bf16[16,48,128]{2,1,0:T(8,128)(2,1)S(1)}, u32[]{:S(2)}, u32[]{:S(2)}) %all-to-all-start) | async-done | bytes 196640 | tf_op jit(solution)/shard_map/gather/all_to_all | solution.py:279
  33.7 5.2 %collective-permute-start.1 = (bf16[8,48,128]{2,1,0:T(8,128)(2,1)S(1)}, bf16[8,48,128]{2,1,0:T(8,128)(2,1)S(1)}, u32[]{:S(2)}, u32[]{:S(2)}) collective-permute-start(bf16[8,48,128]{2,1,0:T(8,128)(2,1)S(1)} %slice.84), channel_id=1, source_target_pairs={{0,450},{2,448},{64,2},{66,0},{128,66},{130,64},{192,130},{194,128... | collective-permute-start | bytes 294920 | tf_op jit(solution)/shard_map/gather/ppermute | solution.py:246
  38.9 2.5 %collective-permute-start = (bf16[8,48,128]{2,1,0:T(8,128)(2,1)S(1)}, bf16[8,48,128]{2,1,0:T(8,128)(2,1)S(1)}, u32[]{:S(2)}, u32[]{:S(2)}) collective-permute-start(bf16[8,48,128]{2,1,0:T(8,128)(2,1)S(1)} %slice.84), channel_id=1, source_target_pairs={{0,448},{64,0},{128,64},{192,128},{256,192},{320,256},{384,320},{4... | collective-permute-start | bytes 294920 | tf_op jit(solution)/shard_map/gather/ppermute | solution.py:240
  41.5 8.6 %all-gather = bf16[64,48,128]{2,1,0:T(8,128)(2,1)S(1)} all-gather(bf16[16,48,128]{2,1,0:T(8,128)(2,1)S(1)} %all-to-all-done), channel_id=2, replica_groups=mesh['region'=8,'z'=16,'yl'=2,'core'=2] {'yl','core'}, dimensions={0}, use_global_device_ids=true | all-gather | bytes 983040 | tf_op jit(solution)/shard_map/gather/all_gather | solution.py:284
  50.1 0.0 copy-done.4
  50.1 0.1 copy.16.off_ref
  50.2 0.0 collective-permute-done.1
  50.2 0.0 collective-permute-done
  50.2 2.1 %all-gather.1 = bf16[4,8,48,128]{3,2,1,0:T(8,128)(2,1)S(1)} all-gather(bf16[2,8,48,128]{3,2,1,0:T(8,128)(2,1)S(1)} %pad_maximum_fusion.1), channel_id=3, replica_groups=mesh['region'=8,'z'=16,'yl'=2,'core'=2] {'core'}, dimensions={0}, use_global_device_ids=true | all-gather | bytes 589824 | tf_op jit(solution)/shard_map/gather/all_gather | solution.py:285
  52.3 0.0 copy-done
  52.3 0.0 copy-done.1
  52.3 0.0 copy-done.2
  52.3 0.0 copy-done.3
  52.3 11.0 %slots.1 = (f32[2,24,48,128]{3,2,1,0:T(8,128)S(1)}, f32[2,24,48,128]{3,2,1,0:T(8,128)S(1)}) custom-call(s32[2]{0:T(128)S(1)} %pad_add_fusion.3.place_ref, s32[1,12,2]{2,1,0:T(8,128)S(1)} %copy.16.off_ref, s32[1,1]{1,0:T(1,128)S(6)} %copy.18.cnt_ref, f32[128,128]{1,0:T(8,128)S(1)} %copy-done.2, f32[128,128]{1,0:T(8,128)S(1)} %copy-done.3, ...), custom_call_target="tpu_custom_call" | custom-call | tf_op jit(solution)/shard_map/slots/pallas_call | solution.py:223
  63.3 2.2 %collective-permute-start.2 = (f32[2,24,48,128]{3,2,1,0:T(8,128)S(1)}, f32[2,24,48,128]{3,2,1,0:T(8,128)S(1)}, u32[]{:S(2)}, u32[]{:S(2)}) collective-permute-start(f32[2,24,48,128]{3,2,1,0:T(8,128)S(1)} %get-tuple-element.23), channel_id=1, source_target_pairs={{0,1},{1,0},{2,3},{3,2},{4,5},{5,4},{6,7},{7,6},{8,9},{9,8},{10,11... | collective-permute-start | bytes 3538952 | tf_op jit(solution)/shard_map/reduce/ppermute | solution.py:235
  65.5 2.5 %collective-permute-done.2 = f32[2,24,48,128]{3,2,1,0:T(8,128)S(1)} collective-permute-done((f32[2,24,48,128]{3,2,1,0:T(8,128)S(1)}, f32[2,24,48,128]{3,2,1,0:T(8,128)S(1)}, u32[]{:S(2)}, u32[]{:S(2)}) %collective-permute-start.2) | collective-permute-done | bytes 1179680 | tf_op jit(solution)/shard_map/reduce/ppermute | solution.py:235
  68.0 0.1 add.19
  68.2 0.1 abs_reduce_fusion
  68.3 0.1 clamp_convert_fusion
  68.5 4.6 %collective-permute-start.4 = (s16[49,8,128]{2,1,0:T(8,128)(2,1)S(1)}, s16[49,8,128]{2,1,0:T(8,128)(2,1)S(1)}, u32[]{:S(2)}, u32[]{:S(2)}) collective-permute-start(s16[49,8,128]{2,1,0:T(8,128)(2,1)S(1)} %get-tuple-element.32), channel_id=1, source_target_pairs={{0,64},{64,128},{128,192},{192,256},{256,320},{320,384},{384,448},... | collective-permute-start | bytes 301064 | tf_op jit(solution)/shard_map/reduce/ppermute | solution.py:240
  73.1 4.2 %collective-permute-start.5 = (s16[49,8,128]{2,1,0:T(8,128)(2,1)S(1)}, s16[49,8,128]{2,1,0:T(8,128)(2,1)S(1)}, u32[]{:S(2)}, u32[]{:S(2)}) collective-permute-start(s16[49,8,128]{2,1,0:T(8,128)(2,1)S(1)} %get-tuple-element.33), channel_id=1, source_target_pairs={{0,66},{2,64},{64,130},{66,128},{128,194},{130,192},{192,258},{194... | collective-permute-start | bytes 301064 | tf_op jit(solution)/shard_map/reduce/ppermute | solution.py:246
  77.4 1.9 %collective-permute-start.3 = (s16[97,8,128]{2,1,0:T(8,128)(2,1)S(1)}, s16[97,8,128]{2,1,0:T(8,128)(2,1)S(1)}, u32[]{:S(2)}, u32[]{:S(2)}) collective-permute-start(s16[97,8,128]{2,1,0:T(8,128)(2,1)S(1)} %pad_add_fusion), channel_id=1, source_target_pairs={{0,2},{2,0},{1,3},{3,1},{4,6},{6,4},{5,7},{7,5},{8,10},{10,8},{9,1... | collective-permute-start | bytes 595976 | tf_op jit(solution)/shard_map/reduce/ppermute | solution.py:235
  79.3 0.0 collective-permute-done.4
  79.3 2.6 %collective-permute-done.5 = s16[49,8,128]{2,1,0:T(8,128)(2,1)S(1)} collective-permute-done((s16[49,8,128]{2,1,0:T(8,128)(2,1)S(1)}, s16[49,8,128]{2,1,0:T(8,128)(2,1)S(1)}, u32[]{:S(2)}, u32[]{:S(2)}) %collective-permute-start.5) | collective-permute-done | bytes 100384 | tf_op jit(solution)/shard_map/reduce/ppermute | solution.py:246
  81.9 0.1 multiply_add_fusion
  82.0 3.7 %collective-permute-done.3 = s16[97,8,128]{2,1,0:T(8,128)(2,1)S(1)} collective-permute-done((s16[97,8,128]{2,1,0:T(8,128)(2,1)S(1)}, s16[97,8,128]{2,1,0:T(8,128)(2,1)S(1)}, u32[]{:S(2)}, u32[]{:S(2)}) %collective-permute-start.3) | collective-permute-done | bytes 198688 | tf_op jit(solution)/shard_map/reduce/ppermute | solution.py:235
  85.7 0.1 convert_multiply_fusion
  85.8 0.1 fusion
  85.9 0.1 clamp_convert_fusion.1
  86.1 21.6 %all_to_all.10 = s16[16,56,128]{2,1,0:T(8,128)(2,1)S(1)} all-to-all(s16[16,56,128]{2,1,0:T(8,128)(2,1)S(1)} %add_bitcast_fusion), channel_id=1, replica_groups=mesh['region'=8,'z'=16,'yl'=2,'core'=2] {'z'}, dimensions={0} | all-to-all | bytes 458752 | tf_op jit(solution)/shard_map/reduce/all_to_all | solution.py:303
  107.7 0.1 multiply_reduce_fusion
  107.8 0.6 slice_bitcast_fusion.3
  (18 shorter events, 0.3 us)
Async XLA Ops:
  0.6 49.4 %copy-start.4 = (s32[1,12,2]{1,2,0:T(2,128)S(1)}, s32[1,12,2]{1,2,0:T(2,128)}, u32[]{:S(2)}) copy-start(s32[1,12,2]{1,2,0:T(2,128)} %param.15) | copy-start | bytes 292
  2.1 31.6 %all-to-all-start = ((bf16[16,48,128]{2,1,0:T(8,128)(2,1)}), bf16[16,48,128]{2,1,0:T(8,128)(2,1)S(1)}, u32[]{:S(2)}, u32[]{:S(2)}) async-start(bf16[16,48,128]{2,1,0:T(8,128)(2,1)} %broadcast_in_dim.4), calls=%async_computation | async-start | bytes 393216 | tf_op jit(solution)/shard_map/gather/all_to_all | solution.py:279
  17.3 35.0 %copy-start = (bf16[4,2,256,256]{3,2,1,0:T(8,128)(2,1)S(1)}, bf16[4,2,256,256]{3,2,1,0:T(8,128)(2,1)}, u32[]{:S(2)}) copy-start(bf16[4,2,256,256]{3,2,1,0:T(8,128)(2,1)} %constant.79.clone.tab_ref) | copy-start | bytes 3145732
  17.3 35.0 %copy-start.1 = (bf16[1,12,128,128]{3,2,1,0:T(8,128)(2,1)S(1)}, bf16[1,12,128,128]{3,2,1,0:T(8,128)(2,1)}, u32[]{:S(2)}) copy-start(bf16[1,12,128,128]{3,2,1,0:T(8,128)(2,1)} %param.14) | copy-start | bytes 1179652
  17.3 35.0 %copy-start.2 = (f32[128,128]{1,0:T(8,128)S(1)}, f32[128,128]{1,0:T(8,128)}, u32[]{:S(2)}) copy-start(f32[128,128]{1,0:T(8,128)} %probe_real_ref.1) | copy-start | bytes 196612
  17.3 35.0 %copy-start.3 = (f32[128,128]{1,0:T(8,128)S(1)}, f32[128,128]{1,0:T(8,128)}, u32[]{:S(2)}) copy-start(f32[128,128]{1,0:T(8,128)} %probe_imag_ref.1) | copy-start | bytes 196612
  33.7 16.5 %collective-permute-start.1 = (bf16[8,48,128]{2,1,0:T(8,128)(2,1)S(1)}, bf16[8,48,128]{2,1,0:T(8,128)(2,1)S(1)}, u32[]{:S(2)}, u32[]{:S(2)}) collective-permute-start(bf16[8,48,128]{2,1,0:T(8,128)(2,1)S(1)} %slice.84), channel_id=1, source_target_pairs={{0,450},{2,448},{64,2},{66,0},{128,66},{130,64},{192,130},{194,128... | collective-permute-start | bytes 294920 | tf_op jit(solution)/shard_map/gather/ppermute | solution.py:246
  38.9 11.3 %collective-permute-start = (bf16[8,48,128]{2,1,0:T(8,128)(2,1)S(1)}, bf16[8,48,128]{2,1,0:T(8,128)(2,1)S(1)}, u32[]{:S(2)}, u32[]{:S(2)}) collective-permute-start(bf16[8,48,128]{2,1,0:T(8,128)(2,1)S(1)} %slice.84), channel_id=1, source_target_pairs={{0,448},{64,0},{128,64},{192,128},{256,192},{320,256},{384,320},{4... | collective-permute-start | bytes 294920 | tf_op jit(solution)/shard_map/gather/ppermute | solution.py:240
  63.3 4.7 %collective-permute-start.2 = (f32[2,24,48,128]{3,2,1,0:T(8,128)S(1)}, f32[2,24,48,128]{3,2,1,0:T(8,128)S(1)}, u32[]{:S(2)}, u32[]{:S(2)}) collective-permute-start(f32[2,24,48,128]{3,2,1,0:T(8,128)S(1)} %get-tuple-element.23), channel_id=1, source_target_pairs={{0,1},{1,0},{2,3},{3,2},{4,5},{5,4},{6,7},{7,6},{8,9},{9,8},{10,11... | collective-permute-start | bytes 3538952 | tf_op jit(solution)/shard_map/reduce/ppermute | solution.py:235
  68.5 10.8 %collective-permute-start.4 = (s16[49,8,128]{2,1,0:T(8,128)(2,1)S(1)}, s16[49,8,128]{2,1,0:T(8,128)(2,1)S(1)}, u32[]{:S(2)}, u32[]{:S(2)}) collective-permute-start(s16[49,8,128]{2,1,0:T(8,128)(2,1)S(1)} %get-tuple-element.32), channel_id=1, source_target_pairs={{0,64},{64,128},{128,192},{192,256},{256,320},{320,384},{384,448},... | collective-permute-start | bytes 301064 | tf_op jit(solution)/shard_map/reduce/ppermute | solution.py:240
  73.1 8.8 %collective-permute-start.5 = (s16[49,8,128]{2,1,0:T(8,128)(2,1)S(1)}, s16[49,8,128]{2,1,0:T(8,128)(2,1)S(1)}, u32[]{:S(2)}, u32[]{:S(2)}) collective-permute-start(s16[49,8,128]{2,1,0:T(8,128)(2,1)S(1)} %get-tuple-element.33), channel_id=1, source_target_pairs={{0,66},{2,64},{64,130},{66,128},{128,194},{130,192},{192,258},{194... | collective-permute-start | bytes 301064 | tf_op jit(solution)/shard_map/reduce/ppermute | solution.py:246
  77.4 8.3 %collective-permute-start.3 = (s16[97,8,128]{2,1,0:T(8,128)(2,1)S(1)}, s16[97,8,128]{2,1,0:T(8,128)(2,1)S(1)}, u32[]{:S(2)}, u32[]{:S(2)}) collective-permute-start(s16[97,8,128]{2,1,0:T(8,128)(2,1)S(1)} %pad_add_fusion), channel_id=1, source_target_pairs={{0,2},{2,0},{1,3},{3,1},{4,6},{6,4},{5,7},{7,5},{8,10},{10,8},{9,1... | collective-permute-start | bytes 595976 | tf_op jit(solution)/shard_map/reduce/ppermute | solution.py:235

commit v6 on v5

--- a/solution.py
+++ b/solution.py
@@ -274,11 +274,15 @@
     scale = 1.0 / math.sqrt(patterns.shape[1] * depth * 4)
 
     with jax.named_scope("gather"):
-        block = jnp.stack([object_real, object_imag]).reshape(2, slices, rows, halves, width)
-        block = block.transpose(1, 3, 0, 2, 4).reshape(packed, width)
-        column = lax.all_to_all(
-            jnp.broadcast_to(block, (depth, packed, width)), "z", 0, 0, tiled=True
-        )
+        parts = [
+            jnp.broadcast_to(
+                part.reshape(slices, rows, halves, width).transpose(0, 2, 1, 3),
+                (depth, slices, halves, rows, width),
+            )
+            for part in (object_real, object_imag)
+        ]
+        block = jnp.stack(parts, axis=3).reshape(depth, packed, width)
+        column = lax.all_to_all(block, "z", 0, 0, tiled=True)
         column, offsets, place = lax.optimization_barrier((column, offsets, place))
         following = jnp.stack([shift(column[:below], -1), shift_and_swap(column[:below], -1)])
         own = lax.all_gather(column, ("yl", "core"), axis=0)

time: 110 us -> 111 us (level)
  Pallas kernels: 11 us -> 6.16 us
  starting transfers between devices: 35.9 us -> 40 us
  blocking collectives: 32.3 us -> 34.4 us
  waiting for transfers between devices: 24.3 us -> 23 us
    ppermute x2, starting transfers between devices: 7.1 us -> 11.9 us  [shift(): lax.ppermute(block, 'region', [(i, (i + distance) % bands) for i in range...]
    pallas_call x1, Pallas kernels: 11 us -> 6.16 us  [slots_call(): pl.pallas_call(functools.partial(slots_kernel, scale), out_shape=[out] *...]
    ppermute x2, starting transfers between devices: 9.44 us -> 7.11 us  [shift_and_swap(): return lax.ppermute(block, ('region', 'yl'), route)]
    all_to_all x1, blocking collectives: 21.6 us -> 23.7 us  [local(): parts = lax.all_to_all(parts, 'z', 0, 0, tiled=True)]
    ppermute x2, waiting for transfers between devices: 6.2 us -> 4.34 us  [swap(): return lax.ppermute(block, axis, [(0, 1), (1, 0)])]
    ppermute x2, starting transfers between devices: 4.14 us -> 5.8 us  [swap(): return lax.ppermute(block, axis, [(0, 1), (1, 0)])]
    reshape x0 -> x2, local copies, waits for them, and re-layouts: none -> 1.41 us  [local(): part.reshape(slices, rows, halves, width).transpose(0, 2, 1, 3)]
where the time goes in v6:
time: 111 us; the launch traced here: 109 us
  starting transfers between devices  40 us (36%)
  blocking collectives  34.4 us (31%)
  waiting for transfers between devices  23 us (21%)
  Pallas kernels  6.16 us (6%)
  local copies, waits for them, and re-layouts  2.32 us (2%)
  other arithmetic  1.81 us (2%)
  between operations  1.68 us (2%)
    all_to_all x1, blocking collectives, local(): parts = lax.all_to_all(parts, 'z', 0, 0, tiled=True)  23.7 us
    all_to_all x1, waiting for transfers between devices, local(): column = lax.all_to_all(block, 'z', 0, 0, tiled=True)  15.5 us
    all_to_all x1, starting transfers between devices, local(): column = lax.all_to_all(block, 'z', 0, 0, tiled=True)  15.2 us
    ppermute x2, starting transfers between devices, shift(): lax.ppermute(block, 'region', [(i, (i + distance) % bands) for i in range...  11.9 us
    all_gather x1, blocking collectives, local(): own = lax.all_gather(column, ('yl', 'core'), axis=0)  8.61 us
    ppermute x2, starting transfers between devices, shift_and_swap(): return lax.ppermute(block, ('region', 'yl'), route)  7.11 us
    pallas_call x1, Pallas kernels, slots_call(): pl.pallas_call(functools.partial(slots_kernel, scale), out_shape=[out] *...  6.16 us
    ppermute x2, starting transfers between devices, swap(): return lax.ppermute(block, axis, [(0, 1), (1, 0)])  5.8 us
  transfers between devices with their start and end apart: 7, of which 4 were waited for; matrix products, arithmetic and copies ran while one was open for 0% of the time, Pallas kernels for 0%

profile of v6, /device:TPU:6, one launch (start us, length us, event | category | flops | bytes accessed | tf_op | source)
XLA Modules:
  0.0 109.5 jit_solution(2715785585345150857)
XLA Ops:
  0.6 0.0 copy-start.4
  0.6 0.7 reshape.146
  1.4 0.7 reshape.147
  2.1 0.8 pad_maximum_fusion.1
  3.0 15.2 %all-to-all-start = ((bf16[16,48,128]{2,1,0:T(8,128)(2,1)}), bf16[16,48,128]{2,1,0:T(8,128)(2,1)S(1)}, u32[]{:S(2)}, u32[]{:S(2)}) async-start(bf16[16,48,128]{2,1,0:T(8,128)(2,1)} %bitcast.2), calls=%async_computation | async-start | bytes 393216 | tf_op jit(solution)/shard_map/gather/all_to_all | solution.py:285
  18.2 0.0 copy-start
  18.2 0.0 copy-start.1
  18.2 0.0 copy-start.2
  18.2 0.0 copy-start.3
  19.0 0.1 pad_add_fusion.3.place_ref
  19.0 15.5 %all-to-all-done = bf16[16,48,128]{2,1,0:T(8,128)(2,1)S(1)} async-done(((bf16[16,48,128]{2,1,0:T(8,128)(2,1)}), bf16[16,48,128]{2,1,0:T(8,128)(2,1)S(1)}, u32[]{:S(2)}, u32[]{:S(2)}) %all-to-all-start) | async-done | bytes 196640 | tf_op jit(solution)/shard_map/gather/all_to_all | solution.py:285
  34.6 5.2 %collective-permute-start.1 = (bf16[8,48,128]{2,1,0:T(8,128)(2,1)S(1)}, bf16[8,48,128]{2,1,0:T(8,128)(2,1)S(1)}, u32[]{:S(2)}, u32[]{:S(2)}) collective-permute-start(bf16[8,48,128]{2,1,0:T(8,128)(2,1)S(1)} %slice.84), channel_id=1, source_target_pairs={{0,450},{2,448},{64,2},{66,0},{128,66},{130,64},{192,130},{194,128... | collective-permute-start | bytes 294920 | tf_op jit(solution)/shard_map/gather/ppermute | solution.py:246
  39.8 2.5 %collective-permute-start = (bf16[8,48,128]{2,1,0:T(8,128)(2,1)S(1)}, bf16[8,48,128]{2,1,0:T(8,128)(2,1)S(1)}, u32[]{:S(2)}, u32[]{:S(2)}) collective-permute-start(bf16[8,48,128]{2,1,0:T(8,128)(2,1)S(1)} %slice.84), channel_id=1, source_target_pairs={{0,448},{64,0},{128,64},{192,128},{256,192},{320,256},{384,320},{4... | collective-permute-start | bytes 294920 | tf_op jit(solution)/shard_map/gather/ppermute | solution.py:240
  42.3 8.6 %all-gather = bf16[64,48,128]{2,1,0:T(8,128)(2,1)S(1)} all-gather(bf16[16,48,128]{2,1,0:T(8,128)(2,1)S(1)} %all-to-all-done), channel_id=2, replica_groups=mesh['region'=8,'z'=16,'yl'=2,'core'=2] {'yl','core'}, dimensions={0}, use_global_device_ids=true | all-gather | bytes 983040 | tf_op jit(solution)/shard_map/gather/all_gather | solution.py:288
  51.0 0.0 copy-done.4
  51.0 0.1 copy.18.off_ref
  51.1 0.0 collective-permute-done.1
  51.1 0.0 collective-permute-done
  51.1 2.1 %all-gather.1 = bf16[4,8,48,128]{3,2,1,0:T(8,128)(2,1)S(1)} all-gather(bf16[2,8,48,128]{3,2,1,0:T(8,128)(2,1)S(1)} %pad_maximum_fusion.2), channel_id=3, replica_groups=mesh['region'=8,'z'=16,'yl'=2,'core'=2] {'core'}, dimensions={0}, use_global_device_ids=true | all-gather | bytes 589824 | tf_op jit(solution)/shard_map/gather/all_gather | solution.py:289
  53.2 0.0 copy-done
  53.2 0.0 copy-done.1
  53.2 0.0 copy-done.2
  53.2 0.0 copy-done.3
  53.2 6.2 %slots.1 = (f32[2,24,48,128]{3,2,1,0:T(8,128)S(1)}, f32[2,24,48,128]{3,2,1,0:T(8,128)S(1)}) custom-call(s32[2]{0:T(128)S(1)} %pad_add_fusion.3.place_ref, s32[1,12,2]{2,1,0:T(8,128)S(1)} %copy.18.off_ref, s32[1,1]{1,0:T(1,128)S(6)} %copy.20.cnt_ref, f32[128,128]{1,0:T(8,128)S(1)} %copy-done.2, f32[128,128]{1,0:T(8,128)S(1)} %copy-done.3, ...), custom_call_target="tpu_custom_call" | custom-call | tf_op jit(solution)/shard_map/slots/pallas_call | solution.py:223
  59.4 2.3 %collective-permute-start.2 = (f32[2,24,48,128]{3,2,1,0:T(8,128)S(1)}, f32[2,24,48,128]{3,2,1,0:T(8,128)S(1)}, u32[]{:S(2)}, u32[]{:S(2)}) collective-permute-start(f32[2,24,48,128]{3,2,1,0:T(8,128)S(1)} %get-tuple-element.23), channel_id=1, source_target_pairs={{0,1},{1,0},{2,3},{3,2},{4,5},{5,4},{6,7},{7,6},{8,9},{9,8},{10,11... | collective-permute-start | bytes 3538952 | tf_op jit(solution)/shard_map/reduce/ppermute | solution.py:235
  61.6 2.5 %collective-permute-done.2 = f32[2,24,48,128]{3,2,1,0:T(8,128)S(1)} collective-permute-done((f32[2,24,48,128]{3,2,1,0:T(8,128)S(1)}, f32[2,24,48,128]{3,2,1,0:T(8,128)S(1)}, u32[]{:S(2)}, u32[]{:S(2)}) %collective-permute-start.2) | collective-permute-done | bytes 1179680 | tf_op jit(solution)/shard_map/reduce/ppermute | solution.py:235
  64.1 0.1 add.19
  64.3 0.1 abs_reduce_fusion
  64.4 0.1 clamp_convert_fusion
  64.6 9.4 %collective-permute-start.4 = (s16[49,8,128]{2,1,0:T(8,128)(2,1)S(1)}, s16[49,8,128]{2,1,0:T(8,128)(2,1)S(1)}, u32[]{:S(2)}, u32[]{:S(2)}) collective-permute-start(s16[49,8,128]{2,1,0:T(8,128)(2,1)S(1)} %get-tuple-element.32), channel_id=1, source_target_pairs={{0,64},{64,128},{128,192},{192,256},{256,320},{320,384},{384,448},... | collective-permute-start | bytes 301064 | tf_op jit(solution)/shard_map/reduce/ppermute | solution.py:240
  74.0 1.9 %collective-permute-start.5 = (s16[49,8,128]{2,1,0:T(8,128)(2,1)S(1)}, s16[49,8,128]{2,1,0:T(8,128)(2,1)S(1)}, u32[]{:S(2)}, u32[]{:S(2)}) collective-permute-start(s16[49,8,128]{2,1,0:T(8,128)(2,1)S(1)} %get-tuple-element.33), channel_id=1, source_target_pairs={{0,66},{2,64},{64,130},{66,128},{128,194},{130,192},{192,258},{194... | collective-permute-start | bytes 301064 | tf_op jit(solution)/shard_map/reduce/ppermute | solution.py:246
  75.9 3.5 %collective-permute-start.3 = (s16[97,8,128]{2,1,0:T(8,128)(2,1)S(1)}, s16[97,8,128]{2,1,0:T(8,128)(2,1)S(1)}, u32[]{:S(2)}, u32[]{:S(2)}) collective-permute-start(s16[97,8,128]{2,1,0:T(8,128)(2,1)S(1)} %pad_add_fusion), channel_id=1, source_target_pairs={{0,2},{2,0},{1,3},{3,1},{4,6},{6,4},{5,7},{7,5},{8,10},{10,8},{9,1... | collective-permute-start | bytes 595976 | tf_op jit(solution)/shard_map/reduce/ppermute | solution.py:235
  79.5 0.0 collective-permute-done.4
  79.5 3.1 %collective-permute-done.5 = s16[49,8,128]{2,1,0:T(8,128)(2,1)S(1)} collective-permute-done((s16[49,8,128]{2,1,0:T(8,128)(2,1)S(1)}, s16[49,8,128]{2,1,0:T(8,128)(2,1)S(1)}, u32[]{:S(2)}, u32[]{:S(2)}) %collective-permute-start.5) | collective-permute-done | bytes 100384 | tf_op jit(solution)/shard_map/reduce/ppermute | solution.py:246
  82.6 0.1 multiply_add_fusion
  82.7 1.9 %collective-permute-done.3 = s16[97,8,128]{2,1,0:T(8,128)(2,1)S(1)} collective-permute-done((s16[97,8,128]{2,1,0:T(8,128)(2,1)S(1)}, s16[97,8,128]{2,1,0:T(8,128)(2,1)S(1)}, u32[]{:S(2)}, u32[]{:S(2)}) %collective-permute-start.3) | collective-permute-done | bytes 198688 | tf_op jit(solution)/shard_map/reduce/ppermute | solution.py:235
  84.6 0.1 convert_multiply_fusion
  84.7 0.1 fusion
  84.9 0.1 clamp_convert_fusion.1
  85.0 23.7 %all_to_all.10 = s16[16,56,128]{2,1,0:T(8,128)(2,1)S(1)} all-to-all(s16[16,56,128]{2,1,0:T(8,128)(2,1)S(1)} %add_bitcast_fusion), channel_id=1, replica_groups=mesh['region'=8,'z'=16,'yl'=2,'core'=2] {'z'}, dimensions={0} | all-to-all | bytes 458752 | tf_op jit(solution)/shard_map/reduce/all_to_all | solution.py:307
  108.8 0.1 multiply_reduce_fusion
  108.8 0.6 slice_bitcast_fusion.3
  (22 shorter events, 0.4 us)
Async XLA Ops:
  0.6 50.3 %copy-start.4 = (s32[1,12,2]{1,2,0:T(2,128)S(1)}, s32[1,12,2]{1,2,0:T(2,128)}, u32[]{:S(2)}) copy-start(s32[1,12,2]{1,2,0:T(2,128)} %param.15) | copy-start | bytes 292
  3.0 31.6 %all-to-all-start = ((bf16[16,48,128]{2,1,0:T(8,128)(2,1)}), bf16[16,48,128]{2,1,0:T(8,128)(2,1)S(1)}, u32[]{:S(2)}, u32[]{:S(2)}) async-start(bf16[16,48,128]{2,1,0:T(8,128)(2,1)} %bitcast.2), calls=%async_computation | async-start | bytes 393216 | tf_op jit(solution)/shard_map/gather/all_to_all | solution.py:285
  18.2 35.0 %copy-start = (bf16[4,2,256,256]{3,2,1,0:T(8,128)(2,1)S(1)}, bf16[4,2,256,256]{3,2,1,0:T(8,128)(2,1)}, u32[]{:S(2)}) copy-start(bf16[4,2,256,256]{3,2,1,0:T(8,128)(2,1)} %constant.79.clone.tab_ref) | copy-start | bytes 3145732
  18.2 35.0 %copy-start.1 = (bf16[1,12,128,128]{3,2,1,0:T(8,128)(2,1)S(1)}, bf16[1,12,128,128]{3,2,1,0:T(8,128)(2,1)}, u32[]{:S(2)}) copy-start(bf16[1,12,128,128]{3,2,1,0:T(8,128)(2,1)} %param.14) | copy-start | bytes 1179652
  18.2 35.0 %copy-start.2 = (f32[128,128]{1,0:T(8,128)S(1)}, f32[128,128]{1,0:T(8,128)}, u32[]{:S(2)}) copy-start(f32[128,128]{1,0:T(8,128)} %probe_real_ref.1) | copy-start | bytes 196612
  18.2 35.0 %copy-start.3 = (f32[128,128]{1,0:T(8,128)S(1)}, f32[128,128]{1,0:T(8,128)}, u32[]{:S(2)}) copy-start(f32[128,128]{1,0:T(8,128)} %probe_imag_ref.1) | copy-start | bytes 196612
  34.6 16.5 %collective-permute-start.1 = (bf16[8,48,128]{2,1,0:T(8,128)(2,1)S(1)}, bf16[8,48,128]{2,1,0:T(8,128)(2,1)S(1)}, u32[]{:S(2)}, u32[]{:S(2)}) collective-permute-start(bf16[8,48,128]{2,1,0:T(8,128)(2,1)S(1)} %slice.84), channel_id=1, source_target_pairs={{0,450},{2,448},{64,2},{66,0},{128,66},{130,64},{192,130},{194,128... | collective-permute-start | bytes 294920 | tf_op jit(solution)/shard_map/gather/ppermute | solution.py:246
  39.8 11.3 %collective-permute-start = (bf16[8,48,128]{2,1,0:T(8,128)(2,1)S(1)}, bf16[8,48,128]{2,1,0:T(8,128)(2,1)S(1)}, u32[]{:S(2)}, u32[]{:S(2)}) collective-permute-start(bf16[8,48,128]{2,1,0:T(8,128)(2,1)S(1)} %slice.84), channel_id=1, source_target_pairs={{0,448},{64,0},{128,64},{192,128},{256,192},{320,256},{384,320},{4... | collective-permute-start | bytes 294920 | tf_op jit(solution)/shard_map/gather/ppermute | solution.py:240
  59.4 4.7 %collective-permute-start.2 = (f32[2,24,48,128]{3,2,1,0:T(8,128)S(1)}, f32[2,24,48,128]{3,2,1,0:T(8,128)S(1)}, u32[]{:S(2)}, u32[]{:S(2)}) collective-permute-start(f32[2,24,48,128]{3,2,1,0:T(8,128)S(1)} %get-tuple-element.23), channel_id=1, source_target_pairs={{0,1},{1,0},{2,3},{3,2},{4,5},{5,4},{6,7},{7,6},{8,9},{9,8},{10,11... | collective-permute-start | bytes 3538952 | tf_op jit(solution)/shard_map/reduce/ppermute | solution.py:235
  64.6 14.9 %collective-permute-start.4 = (s16[49,8,128]{2,1,0:T(8,128)(2,1)S(1)}, s16[49,8,128]{2,1,0:T(8,128)(2,1)S(1)}, u32[]{:S(2)}, u32[]{:S(2)}) collective-permute-start(s16[49,8,128]{2,1,0:T(8,128)(2,1)S(1)} %get-tuple-element.32), channel_id=1, source_target_pairs={{0,64},{64,128},{128,192},{192,256},{256,320},{320,384},{384,448},... | collective-permute-start | bytes 301064 | tf_op jit(solution)/shard_map/reduce/ppermute | solution.py:240
  74.0 8.6 %collective-permute-start.5 = (s16[49,8,128]{2,1,0:T(8,128)(2,1)S(1)}, s16[49,8,128]{2,1,0:T(8,128)(2,1)S(1)}, u32[]{:S(2)}, u32[]{:S(2)}) collective-permute-start(s16[49,8,128]{2,1,0:T(8,128)(2,1)S(1)} %get-tuple-element.33), channel_id=1, source_target_pairs={{0,66},{2,64},{64,130},{66,128},{128,194},{130,192},{192,258},{194... | collective-permute-start | bytes 301064 | tf_op jit(solution)/shard_map/reduce/ppermute | solution.py:246
  75.9 8.7 %collective-permute-start.3 = (s16[97,8,128]{2,1,0:T(8,128)(2,1)S(1)}, s16[97,8,128]{2,1,0:T(8,128)(2,1)S(1)}, u32[]{:S(2)}, u32[]{:S(2)}) collective-permute-start(s16[97,8,128]{2,1,0:T(8,128)(2,1)S(1)} %pad_add_fusion), channel_id=1, source_target_pairs={{0,2},{2,0},{1,3},{3,1},{4,6},{6,4},{5,7},{7,5},{8,10},{10,8},{9,1... | collective-permute-start | bytes 595976 | tf_op jit(solution)/shard_map/reduce/ppermute | solution.py:235
